TPU v7x, 768 devices: a whole 4x8x12 slice. The times are simulated.
768 devices in a mesh: row: 192 (over y, x, z_lo), col: 4 (over z_hi, core).
Axes of the slice: x: 4, y: 8, z: 12 (z_hi: 2, z_lo: 6; z = z_hi * 6 + z_lo), core: 2. Of those that a mesh axis runs over, the one named last changes fastest.
Arguments:
- start_rows: bfloat16 [98304, 128], P('row'), may hold values from -3 to 3
- col_factors: bfloat16 [24576, 128], P(('row', 'col')), as said below
- block_rows: int32 [192, 4, 32], P('row', 'col'), may hold values from 0 to 3
- block_cols: int32 [192, 4, 32], P('row', 'col'), may hold values from 0 to 47
- block_masks: int32 [192, 4, 32, 128, 128], P('row', 'col'), may hold values 0 or 1
- block_counts: int32 [192, 4], P('row', 'col'), may hold values from 1 to 32, as said below
Outputs:
- solution: bfloat16 [98304, 128], P(('row', 'col'))
- residual: float32 [98304, 128], P(('row', 'col'))
Inputs may be any that keep to these rules, and one draw needn't show every extreme that they name: `block_counts`: entries past a list's count are ignored; in every draw some list has exactly 32 live slots. `col_factors`: column factor rows have scales spread over a wide range.
All inputs are finite; a program needn't handle non-finite values. No bound on the sum of `block_masks` on one device may be relied on, other than what follows from the above.
Results may differ from a plain program's by a relative error of at most 0.04.
Values may be sent and summed in bfloat16 or wider, within the bound.
No kernel may reach another device: no remote copies, remote signals or barrier semaphores. Data moves between devices by JAX's collectives and lax.ppermute only.
A program may use at most 32 MiB of HBM per device.

v0:
```python
import jax
import jax.numpy as jnp
from jax import lax
from jax.sharding import PartitionSpec as P

ITERS = 3


CONFIDENCE = 2.0
REGULARIZE = 0.5
EPSILON = 1e-06


def block_sum(factor, col_shard, row_ids, col_ids, edge_masks, live_count, opening):
    slots = row_ids.shape[0]
    height = edge_masks.shape[-1]
    width = factor.shape[1]
    row_blocks = factor.reshape(-1, height, width)[row_ids]
    col_blocks = col_shard.reshape(-1, height, width)[col_ids]
    scores = jnp.einsum("nik,njk->nij", row_blocks, col_blocks, preferred_element_type=jnp.float32)
    live = ((jnp.arange(slots) < live_count)[:, None, None] & (edge_masks > 0)).astype(jnp.float32)
    if opening:
        weights = (1.0 + CONFIDENCE - CONFIDENCE * scores) * live
    else:
        weights = CONFIDENCE * scores * live
    weights = weights.astype(jnp.bfloat16)
    terms = jnp.einsum("nij,njk->nik", weights, col_blocks, preferred_element_type=jnp.float32)
    placer = (row_ids[None, :] == jnp.arange(factor.shape[0] // height)[:, None]).astype(
        jnp.float32
    )
    return jnp.einsum("rn,nik->rik", placer, terms).reshape(factor.shape[0], width)


def per_device(start_rows, col_factors, block_rows, block_cols, block_masks, block_counts):
    col_shard = lax.all_gather(col_factors, "row", axis=0, tiled=True)
    gravity = start_rows.shape[1] / (col_shard.shape[0] * lax.axis_size("col"))
    contract = (((0,), (0,)), ((), ()))
    gramian = lax.psum(
        lax.dot_general(col_factors, col_factors, contract, preferred_element_type=jnp.float32),
        ("row", "col"),
    )
    row_ids = block_rows[0, 0]
    col_ids = block_cols[0, 0]
    edge_masks = block_masks[0, 0]
    live_count = block_counts[0, 0]
    share_rows = start_rows.shape[0] // lax.axis_size("col")
    offset = lax.axis_index("col") * share_rows

    def dense(matrix):
        return (
            gravity * jnp.dot(matrix, gramian, precision=lax.Precision.HIGHEST)
            + REGULARIZE * matrix
        )

    def sparse_part(factor, opening):
        return block_sum(factor, col_shard, row_ids, col_ids, edge_masks, live_count, opening)

    def combine_terms(partial_value):
        return lax.psum(partial_value, "col")

    solution = start_rows.astype(jnp.float32)
    initial = combine_terms(sparse_part(start_rows, True))
    residual = initial - dense(solution)
    direction = residual
    norm_now = jnp.sum(residual * residual, axis=1, keepdims=True)
    for step in range(ITERS):
        image = dense(direction) + combine_terms(sparse_part(direction.astype(jnp.bfloat16), False))
        step_size = norm_now / (jnp.sum(direction * image, axis=1, keepdims=True) + EPSILON)
        solution = solution + step_size * direction
        residual = residual - step_size * image
        norm_next = jnp.sum(residual * residual, axis=1, keepdims=True)
        direction = residual + norm_next / (norm_now + EPSILON) * direction
        norm_now = norm_next
    solution = lax.dynamic_slice_in_dim(solution, offset, share_rows, 0)
    residual = lax.dynamic_slice_in_dim(residual, offset, share_rows, 0)
    return (solution.astype(jnp.bfloat16), residual)


def solution(mesh):
    placed = (
        P("row", None),
        P(("row", "col"), None),
        P("row", "col", None),
        P("row", "col", None),
        P("row", "col", None, None, None),
        P("row", "col"),
    )
    return jax.shard_map(
        per_device,
        mesh=mesh,
        in_specs=placed,
        out_specs=(P(("row", "col"), None), P(("row", "col"), None)),
        check_vma=False,
    )
```

profile of v0, /device:TPU:1, one launch (start us, length us, event | category | flops | bytes accessed | tf_op | source)
XLA Modules:
  0.0 1616.3 jit_solution(10224686207913472461)
XLA Ops:
  8.8 1.6 fusion.49
  12.4 1.7 gather_fusion
  14.1 2.0 bitcast_and_fusion
  16.1 1144.8 %all-gather.2.cloned.1.call-done = bf16[6144,128]{1,0:T(8,128)(2,1)} async-done(((bf16[32,128]{1,0:T(8,128)(2,1)}), bf16[6144,128]{1,0:T(8,128)(2,1)}) %all-gather.2.cloned.1.call-update) | async-done | bytes 1572880 | tf_op jit(solution)/shard_map/all_gather | solution.py:35
  1160.9 2.2 gather_fusion.1
  1163.0 2.1 fusion.2
  1165.2 1.9 fusion
  1167.1 0.8 copy.18
  1168.2 207.3 %all-reduce.6.cloned.1.call-done = f32[512,128]{0,1:T(8,128)} async-done(((f32[512,128]{0,1:T(8,128)}), f32[512,128]{0,1:T(8,128)}) %all-reduce.6.cloned.1.call-update) | async-done | bytes 262160 | tf_op jit(solution)/shard_map/psum | solution.py:59
  1375.5 1.3 fusion.48
  1377.0 0.7 gather_fusion.2
  1377.7 2.1 fusion.3
  1379.9 2.0 copy.32
  1382.1 0.7 copy.57
  1382.9 68.7 %all-reduce.10.cloned.1.call-done = f32[512,128]{0,1:T(8,128)} async-done(((f32[512,128]{0,1:T(8,128)}), f32[512,128]{0,1:T(8,128)}) %all-reduce.10.cloned.1.call-update) | async-done | bytes 262160 | tf_op jit(solution)/shard_map/psum | solution.py:59
  1451.6 1.4 multiply_reduce_fusion.4
  1453.3 0.8 gather_fusion.3
  1454.1 2.1 fusion.4
  1456.2 2.0 copy.36
  1458.4 0.7 copy.56
  1459.2 68.8 %all-reduce.12.cloned.1.call-done = f32[512,128]{0,1:T(8,128)} async-done(((f32[512,128]{0,1:T(8,128)}), f32[512,128]{0,1:T(8,128)}) %all-reduce.12.cloned.1.call-update) | async-done | bytes 262160 | tf_op jit(solution)/shard_map/psum | solution.py:59
  1528.0 1.4 multiply_reduce_fusion.2
  1530.2 0.7 gather_fusion.4
  1530.9 2.1 fusion.5
  1533.1 2.0 copy.39
  1535.3 0.7 copy.55
  1536.2 0.8 dynamic-slice.1
  1536.9 67.9 %all-reduce.14.cloned.1.call-done = f32[512,128]{0,1:T(8,128)} async-done(((f32[512,128]{0,1:T(8,128)}), f32[512,128]{0,1:T(8,128)}) %all-reduce.14.cloned.1.call-update) | async-done | bytes 262160 | tf_op jit(solution)/shard_map/psum | solution.py:59
  1604.8 1.4 multiply_reduce_fusion
  1606.3 0.9 dynamic-slice_subtract_fusion
  1607.2 0.7 copy.28
  1608.0 0.7 copy.27
  (58 shorter events, 4.6 us)
Async XLA Ops:
  8.0 1152.9 %all-gather.2.cloned.1.call-start = ((), (), s32[]{:S(2)}) async-start(), calls=%async_computation | async-start | bytes 1581056 | tf_op jit(solution)/shard_map/all_gather | solution.py:35
  8.7 1159.4 %all-reduce.8.cloned.1.call-start = ((), (), s32[]{:S(2)}) async-start(), calls=%async_computation.2 | async-start | bytes 131072 | tf_op jit(solution)/shard_map/psum | solution.py:38
  10.4 1365.1 %all-reduce.6.cloned.1.call-start = ((), (), s32[]{:S(2)}) async-start(), calls=%async_computation.1 | async-start | bytes 524288 | tf_op jit(solution)/shard_map/psum | solution.py:59
  1163.0 2.1 copy-start.7
  1165.2 2.9 copy-start
  1168.0 283.7 %all-reduce.10.cloned.1.call-start = ((), (), s32[]{:S(2)}) async-start(), calls=%async_computation.3 | async-start | bytes 524288 | tf_op jit(solution)/shard_map/psum | solution.py:59
  1168.1 208.8 %copy-start.2 = (bf16[512,128]{0,1:T(8,128)(2,1)}, bf16[512,128]{0,1:T(8,128)(2,1)S(1)}, u32[]{:S(2)}) copy-start(bf16[512,128]{0,1:T(8,128)(2,1)S(1)} %copy.16) | copy-start | bytes 393220
  1379.9 71.8 %copy-start.4 = (f32[128,128]{1,0:T(8,128)S(1)}, f32[128,128]{1,0:T(8,128)}, u32[]{:S(2)}) copy-start(f32[128,128]{1,0:T(8,128)} %all-reduce.8.cloned.1.call-done) | copy-start | bytes 196612
  1382.8 145.1 %all-reduce.12.cloned.1.call-start = ((), (), s32[]{:S(2)}) async-start(), calls=%async_computation.4 | async-start | bytes 524288 | tf_op jit(solution)/shard_map/psum | solution.py:59
  1456.2 71.8 %copy-start.5 = (f32[128,128]{1,0:T(8,128)S(1)}, f32[128,128]{1,0:T(8,128)}, u32[]{:S(2)}) copy-start(f32[128,128]{1,0:T(8,128)} %all-reduce.8.cloned.1.call-done) | copy-start | bytes 196612
  1459.1 145.7 %all-reduce.14.cloned.1.call-start = ((), (), s32[]{:S(2)}) async-start(), calls=%async_computation.5 | async-start | bytes 524288 | tf_op jit(solution)/shard_map/psum | solution.py:59
  1529.4 0.6 copy-start.9
  1529.5 0.7 copy-start.1
  1533.1 2.0 copy-start.8
  1533.1 3.0 copy-start.3
  1533.1 71.8 %copy-start.6 = (f32[128,128]{1,0:T(8,128)S(1)}, f32[128,128]{1,0:T(8,128)}, u32[]{:S(2)}) copy-start(f32[128,128]{1,0:T(8,128)} %all-reduce.8.cloned.1.call-done) | copy-start | bytes 196612
Sparse Core Ops, SparseCore 0:
  11.5 1149.3 all-gather.1
Sparse Core Ops, SparseCore 1:
  15.2 465.2 all-reduce.7
  1168.0 207.4 all-reduce.5
  1382.9 68.7 all-reduce.9
  1459.2 68.7 all-reduce.11
  1536.1 68.7 all-reduce.13
where the time goes:
time: 1620 us
  waiting for transfers between devices  1560 us (96%)
  matrix products  18.3 us (1%)
  local copies, waits for them, and re-layouts  18.3 us (1%)
  between operations  16.6 us (1%)
    all_gather x1, waiting for transfers between devices, per_device(): col_shard = lax.all_gather(col_factors, 'row', axis=0, tiled=True)  1140 us
    psum x4, waiting for transfers between devices, combine_terms(): return lax.psum(partial_value, 'col')  413 us
  transfers between devices with their start and end apart: 6, of which 5 were waited for; matrix products, arithmetic and copies ran while one was open for 1% of the time, Pallas kernels for 0%

commit v1 on v0

v1 whole, which is shorter than its diff:
```python
import jax
import jax.numpy as jnp
from jax import lax
from jax.experimental import pallas as pl
from jax.experimental.pallas import tpu as pltpu
from jax.sharding import Mesh, PartitionSpec as P

ITERS = 3
CONFIDENCE = 2.0
REGULARIZE = 0.5
EPSILON = 1e-06

ROW = ("y", "x", "zl")
COL = ("zh", "core")
SIZES = {"y": 8, "x": 4, "zl": 6, "zh": 2, "core": 2}

BLK = 128
K = 128
NB = 32
PIECE = 2 * BLK
STRIDE = NB
TRIPS = 4 * STRIDE
SHIFT = 64
VMEM_LIMIT = 40 * 1024 * 1024


def lists_kernel(ids_ref, out_ref):
    core = lax.axis_index("core")

    def clear(i, carry):
        out_ref[i] = NB * SHIFT
        return carry

    lax.fori_loop(0, 4 * STRIDE, clear, 0, unroll=8)
    longest = jnp.int32(0)
    for group in range(2):
        holder = core if group == 0 else 1 - core
        live = ids_ref[holder, 2 * NB]

        def place(slot, ends, holder=holder, group=group):
            low, high = ends
            row = ids_ref[holder, slot]
            entry = slot * SHIFT + ids_ref[holder, NB + slot]
            mine = lax.rem(row, 2) == core
            upper = row >= 2

            @pl.when(mine)
            def _():
                out_ref[jnp.where(upper, (2 * group + 1) * STRIDE + high, 2 * group * STRIDE + low)] = entry

            low = low + jnp.where(mine & jnp.logical_not(upper), 1, 0)
            high = high + jnp.where(mine & upper, 1, 0)
            return low, high

        low, high = lax.fori_loop(0, live, place, (jnp.int32(0), jnp.int32(0)))
        longest = jnp.maximum(longest, jnp.maximum(low, high))
    out_ref[TRIPS] = lax.div(longest + 1, 2)


def gram_of(v_ref):
    step = 512

    def body(i, total):
        block = v_ref[pl.ds(pl.multiple_of(i * step, step), step), :]
        return total + lax.dot_general(
            block, block, (((0,), (0,)), ((), ())), preferred_element_type=jnp.float32
        )

    return lax.fori_loop(0, v_ref.shape[0] // step, body, jnp.zeros((K, K), jnp.float32))


def gram_kernel(v_ref, out_ref):
    out_ref[...] = gram_of(v_ref)


def add_sparse(lists_ref, x_ref, v_refs, m_refs, out_ref, opening):
    def body(i, carry):
        for r in range(2):
            cols = []
            masks = []
            for g in range(2):
                for k in range(2):
                    entry = lists_ref[(2 * g + r) * STRIDE + 2 * i + k]
                    slot = lax.div(entry, SHIFT)
                    start = pl.multiple_of(lax.rem(entry, SHIFT) * BLK, BLK)
                    cols.append(v_refs[g][pl.ds(start, BLK), :])
                    masks.append(m_refs[g][slot])
            block = jnp.concatenate(cols, axis=0)
            mask = jnp.concatenate(masks, axis=1)
            rows = x_ref[pl.ds(r * BLK, BLK), :]
            scores = lax.dot_general(
                rows, block, (((1,), (1,)), ((), ())), preferred_element_type=jnp.float32
            )
            if opening:
                scores = (1.0 + CONFIDENCE) / CONFIDENCE - scores
            weights = scores.astype(jnp.bfloat16) * mask
            out_ref[pl.ds(r * BLK, BLK), :] += jnp.dot(
                weights, block, preferred_element_type=jnp.float32
            )
        return carry

    lax.fori_loop(0, lists_ref[TRIPS], body, 0)


def exact_dot(a, b):
    return jnp.dot(a, b, precision=lax.Precision.HIGHEST, preferred_element_type=jnp.float32)


def init_kernel(gravity, lists_ref, x_ref, v0, v1, m0, m1, own_gram, part_ref, gram_ref):
    gram = gravity * (own_gram[...] + gram_of(v1))
    gram_ref[...] = gram
    part_ref[...] = -exact_dot(x_ref[...].astype(jnp.float32), gram)
    add_sparse(lists_ref, x_ref, (v0, v1), (m0, m1), part_ref, True)


def row_sum(a):
    return jnp.sum(a, axis=1, keepdims=True)


def advance(both, direction, residual, sol):
    image = both + REGULARIZE * direction
    norm_now = row_sum(residual * residual)
    step = norm_now / (row_sum(direction * image) + EPSILON)
    sol = sol + step * direction
    residual = residual - step * image
    return sol, residual, norm_now


def image_part(lists_ref, d, low_ref, v0, v1, m0, m1, gram_ref, part_ref):
    low_ref[...] = d.astype(jnp.bfloat16)
    part_ref[...] = exact_dot(d, gram_ref[...])
    add_sparse(lists_ref, low_ref, (v0, v1), (m0, m1), part_ref, False)


def start_kernel(lists_ref, both_ref, x_ref, v0, v1, m0, m1, gram_ref, res_ref, part_ref, low_ref):
    residual = both_ref[:PIECE] + both_ref[PIECE:] - REGULARIZE * x_ref[...].astype(jnp.float32)
    res_ref[...] = residual
    image_part(lists_ref, residual, low_ref, v0, v1, m0, m1, gram_ref, part_ref)


def step_kernel(
    lists_ref, both_ref, sol_in, res_in, dir_in, v0, v1, m0, m1, gram_ref,
    sol_ref, res_ref, dir_ref, part_ref, low_ref,
):
    direction = dir_in[...]
    sol, residual, norm_now = advance(
        both_ref[:PIECE] + both_ref[PIECE:], direction, res_in[...], sol_in[...].astype(jnp.float32)
    )
    sol_ref[...] = sol
    res_ref[...] = residual
    direction = residual + row_sum(residual * residual) / (norm_now + EPSILON) * direction
    dir_ref[...] = direction
    image_part(lists_ref, direction, low_ref, v0, v1, m0, m1, gram_ref, part_ref)


def last_kernel(both_ref, sol_in, res_in, dir_in, sol_ref, res_ref):
    start = pl.multiple_of(lax.axis_index("zh") * BLK, BLK)
    mine = pl.ds(start, BLK)
    both = both_ref[mine, :] + both_ref[pl.ds(start + PIECE, BLK), :]
    sol, residual, _ = advance(both, dir_in[mine, :], res_in[mine, :], sol_in[mine, :])
    sol_ref[...] = sol.astype(jnp.bfloat16)
    res_ref[...] = residual


def on_chip(kernel, args, outs, scratch=(), smem=1):
    vmem = pl.BlockSpec(memory_space=pltpu.VMEM)
    scalar = pl.BlockSpec(memory_space=pltpu.SMEM)
    return pl.pallas_call(
        kernel,
        out_shape=[jax.ShapeDtypeStruct(shape, dtype) for shape, dtype in outs],
        in_specs=[scalar] * smem + [vmem] * (len(args) - smem),
        out_specs=[vmem] * len(outs),
        scratch_shapes=list(scratch),
        compiler_params=pltpu.CompilerParams(vmem_limit_bytes=VMEM_LIMIT),
    )(*args)


def gather_by_exchange(block, axes):
    count = 1
    for axis in axes:
        count *= SIZES[axis]
    sent = jnp.broadcast_to(block[None], (count,) + block.shape)
    got = lax.all_to_all(sent, axes, 0, 0, tiled=True)
    return got.reshape(count * block.shape[0], block.shape[1])


def swap(value):
    return lax.ppermute(value, "core", [(0, 1), (1, 0)])


def per_device(start_rows, col_factors, block_rows, block_cols, block_masks, block_counts):
    f32, bf16 = jnp.float32, jnp.bfloat16
    core = lax.axis_index("core")
    gravity = K / (col_factors.shape[0] * 768)

    live = (jnp.arange(NB + 1) < block_counts[0, 0])[:, None, None]
    padded = jnp.pad(block_masks[0, 0], ((0, 1), (0, 0), (0, 0)))
    own_masks = jnp.where(live & (padded > 0), CONFIDENCE, 0.0).astype(bf16)
    other_masks = swap(own_masks)

    ids = jnp.concatenate(
        [block_rows[0, 0], block_cols[0, 0], jnp.broadcast_to(block_counts[0, 0], (2 * NB,))]
    )[None]
    ids = lax.all_gather(ids, "core", axis=0, tiled=True)
    lists = pl.pallas_call(
        lists_kernel,
        out_shape=jax.ShapeDtypeStruct((2 * TRIPS,), jnp.int32),
        in_specs=[pl.BlockSpec(memory_space=pltpu.SMEM)],
        out_specs=pl.BlockSpec(memory_space=pltpu.SMEM),
    )(ids)

    own = gather_by_exchange(gather_by_exchange(col_factors, ("zl",)), ("y", "x"))
    other = swap(own)
    (own_gram,) = on_chip(gram_kernel, (own,), [((K, K), f32)], smem=0)

    rows = lax.dynamic_slice_in_dim(start_rows.reshape(2, 2, BLK, K), core, 1, 1).reshape(PIECE, K)
    big = (own, other, own_masks, other_masks)
    whole = ((PIECE, K), f32)
    low = (pltpu.VMEM((PIECE, K), bf16),)

    def both(part):
        return lax.all_gather(part, "zh", axis=0, tiled=True)

    part, gram = on_chip(
        lambda *refs: init_kernel(gravity, *refs), (lists, rows) + big + (own_gram,), [whole, ((K, K), f32)]
    )
    residual, part = on_chip(
        start_kernel, (lists, both(part), rows) + big + (gram,), [whole] * 2, low
    )
    sol, direction = rows, residual
    for _ in range(ITERS - 1):
        sol, residual, direction, part = on_chip(
            step_kernel, (lists, both(part), sol, residual, direction) + big + (gram,), [whole] * 4, low
        )
    return tuple(
        on_chip(
            last_kernel, (both(part), sol, residual, direction), [((BLK, K), bf16), ((BLK, K), f32)], smem=0
        )
    )


def solution(mesh):
    fine = Mesh(mesh.devices.reshape(tuple(SIZES.values())), tuple(SIZES))
    placed = (
        P(ROW, None),
        P(ROW + COL, None),
        P(ROW, COL, None),
        P(ROW, COL, None),
        P(ROW, COL, None, None, None),
        P(ROW, COL),
    )
    return jax.shard_map(
        per_device,
        mesh=fine,
        in_specs=placed,
        out_specs=(P(ROW + COL, None), P(ROW + COL, None)),
        check_vma=False,
    )
```

time: 1620 us -> 169 us (0.10)
  the two profiles are of different devices: /device:TPU:1 before, /device:TPU:9 now
where the time goes in v1:
time: 169 us; the launch traced here: 168 us
  blocking collectives  138 us (82%)
  Pallas kernels  18.1 us (11%)
  starting transfers between devices  8.63 us (5%)
  local copies, waits for them, and re-layouts  1.8 us (1%)
    all_gather x4, blocking collectives, both(): return lax.all_gather(part, 'zh', axis=0, tiled=True)  70.1 us
    all_to_all x2, blocking collectives, gather_by_exchange(): got = lax.all_to_all(sent, axes, 0, 0, tiled=True)  65 us
    pallas_call x6, Pallas kernels, on_chip(): pl.pallas_call(kernel, out_shape=[jax.ShapeDtypeStruct(shape, dtype) for...  16.5 us
    ppermute x2, starting transfers between devices, swap(): return lax.ppermute(value, 'core', [(0, 1), (1, 0)])  8.63 us
  transfers between devices with their start and end apart: 2, of which 0 were waited for; matrix products, arithmetic and copies ran while one was open for 0% of the time, Pallas kernels for 3%

profile of v1, /device:TPU:9, one launch (start us, length us, event | category | flops | bytes accessed | tf_op | source)
XLA Modules:
  0.0 168.4 jit_solution(13848425814352684722)
XLA Ops:
  0.6 0.0 copy-start
  0.6 0.7 broadcast_in_dim.30
  1.4 19.2 %all_to_all.10 = bf16[6,32,128]{2,1,0:T(8,128)(2,1)S(1)} all-to-all(bf16[6,32,128]{2,1,0:T(8,128)(2,1)S(1)} %broadcast_in_dim.30), channel_id=1, replica_groups=mesh['y'=8,'x'=4,'zl'=6,'zh'=2,'core'=2] {'zl'}, dimensions={0} | all-to-all | bytes 98304 | tf_op jit(solution)/shard_map/all_to_all | solution.py:183
  20.6 0.0 copy-start.3
  20.6 0.3 broadcast_in_dim.32
  20.9 45.8 %all_to_all.11 = bf16[32,192,128]{2,1,0:T(8,128)(2,1)S(1)} all-to-all(bf16[32,192,128]{2,1,0:T(8,128)(2,1)S(1)} %broadcast_in_dim.32), channel_id=1, replica_groups=mesh['y'=8,'x'=4,'zl'=6,'zh'=2,'core'=2] {'y','x'}, dimensions={0} | all-to-all | bytes 3145728 | tf_op jit(solution)/shard_map/all_to_all | solution.py:183
  66.8 0.0 copy-start.4
  66.8 6.7 %collective-permute-start = (bf16[6144,128]{1,0:T(8,128)(2,1)S(1)}, bf16[6144,128]{1,0:T(8,128)(2,1)}, u32[]{:S(2)}, u32[]{:S(2)}) collective-permute-start(bf16[6144,128]{1,0:T(8,128)(2,1)S(1)} %bitcast.16), channel_id=1, source_target_pairs={{0,1},{1,0},{2,3},{3,2},{4,5},{5,4},{6,7},{7,6},{8,9},{9,8},{10,11... | collective-permute-start | bytes 4718600 | tf_op jit(solution)/shard_map/ppermute | solution.py:188
  74.2 0.0 copy-done.3
  74.2 0.4 select_convert_fusion.refs_4_.m0
  74.6 1.9 %collective-permute-start.1 = (bf16[33,128,128]{2,1,0:T(8,128)(2,1)S(1)}, bf16[33,128,128]{2,1,0:T(8,128)(2,1)}, u32[]{:S(2)}, u32[]{:S(2)}) collective-permute-start(bf16[33,128,128]{2,1,0:T(8,128)(2,1)S(1)} %select_convert_fusion.refs_4_.m0), channel_id=1, source_target_pairs={{0,1},{1,0},{2,3},{3,2},{4,5},{5,4},{6,7},{7,6},{8,9},{9,8},{10,11... | collective-permute-start | bytes 3244040 | tf_op jit(solution)/shard_map/ppermute | solution.py:188
  76.6 0.0 copy-done.4
  76.6 0.0 copy-done.5
  76.6 0.1 add_bitcast_fusion
  76.7 2.7 %all-gather.1 = s32[2,1,128]{2,1,0:T(1,128)} all-gather(s32[1,1,128]{2,1,0:T(1,128)S(1)} %add_bitcast_fusion), channel_id=2, replica_groups=mesh['y'=8,'x'=4,'zl'=6,'zh'=2,'core'=2] {'core'}, dimensions={0}, use_global_device_ids=true | all-gather | bytes 1536 | tf_op jit(solution)/shard_map/all_gather | solution.py:204
  79.4 1.6 shard_map.77.refs_0_.lists_ref
  81.0 0.0 copy-done
  81.0 2.8 %shard_map.78.refs_6_ = f32[128,128]{1,0:T(8,128)S(1)} custom-call(bf16[6144,128]{1,0:T(8,128)(2,1)S(1)} %bitcast.17), custom_call_target="tpu_custom_call" | custom-call | tf_op jit(solution)/shard_map/pallas_call | solution.py:168
  83.8 0.0 collective-permute-done.1.refs_5_.m1
  83.8 0.0 collective-permute-done.refs_3_.v1
  83.8 0.0 copy-start.1
  83.8 0.7 copy-done.1
  84.5 5.3 %shard_map.79 = (f32[256,128]{1,0:T(8,128)S(1)}, f32[128,128]{1,0:T(8,128)S(1)}) custom-call(s32[256]{0:T(256)S(1)} %copy-done.1, bf16[256,128]{1,0:T(8,128)(2,1)S(1)} %bitcast.22, bf16[6144,128]{1,0:T(8,128)(2,1)S(1)} %bitcast.18, bf16[6144,128]{1,0:T(8,128)(2,1)} %collective-permute-done.refs_3_.v1, ...), custom_call_target="tpu_custom_call" | custom-call | tf_op jit(solution)/shard_map/pallas_call | solution.py:168
  89.8 19.8 %all_gather.16.both_ref = f32[512,128]{1,0:T(8,128)S(1)} all-gather(f32[256,128]{1,0:T(8,128)S(1)} %get-tuple-element.14), channel_id=1, replica_groups=mesh['y'=8,'x'=4,'zl'=6,'zh'=2,'core'=2] {'zh'}, dimensions={0}, use_global_device_ids=true | all-gather | bytes 393216 | tf_op jit(solution)/shard_map/all_gather | solution.py:222
  109.5 0.0 copy-done.2
  109.5 2.5 %shard_map.80 = (f32[256,128]{1,0:T(8,128)S(1)}, f32[256,128]{1,0:T(8,128)S(1)}) custom-call(s32[256]{0:T(256)S(1)} %copy-done.2, f32[512,128]{1,0:T(8,128)S(1)} %all_gather.16.both_ref, bf16[256,128]{1,0:T(8,128)(2,1)S(1)} %bitcast.23, bf16[6144,128]{1,0:T(8,128)(2,1)S(1)} %bitcast.19, bf16[6144,128]{1,0:T(8,128)(2,1)} %collective-permute-done.refs_3_.v1, ...), custom_call_target="tpu_custom_call" | custom-call | tf_op jit(solution)/shard_map/pallas_call | solution.py:168
  112.0 17.3 %all_gather.17.both_ref = f32[512,128]{1,0:T(8,128)S(1)} all-gather(f32[256,128]{1,0:T(8,128)S(1)} %get-tuple-element.16), channel_id=1, replica_groups=mesh['y'=8,'x'=4,'zl'=6,'zh'=2,'core'=2] {'zh'}, dimensions={0}, use_global_device_ids=true | all-gather | bytes 393216 | tf_op jit(solution)/shard_map/all_gather | solution.py:222
  129.3 2.6 %shard_map.81 = (f32[256,128]{1,0:T(8,128)S(1)}, f32[256,128]{1,0:T(8,128)S(1)}, f32[256,128]{1,0:T(8,128)S(1)}, f32[256,128]{1,0:T(8,128)S(1)}) custom-call(s32[256]{0:T(256)S(1)} %copy-done.2, f32[512,128]{1,0:T(8,128)S(1)} %all_gather.17.both_ref, bf16[256,128]{1,0:T(8,128)(2,1)S(1)} %bitcast.24, f32[256,128]{1,0:T(8,128)S(1)} %get-tuple-element.17.res_in.dir_in, ...), custom_call_target="tpu_custom_call" | custom-call | tf_op jit(solution)/shard_map/pallas_call | solution.py:168
  131.9 16.6 %all_gather.18.both_ref = f32[512,128]{1,0:T(8,128)S(1)} all-gather(f32[256,128]{1,0:T(8,128)S(1)} %get-tuple-element.18), channel_id=1, replica_groups=mesh['y'=8,'x'=4,'zl'=6,'zh'=2,'core'=2] {'zh'}, dimensions={0}, use_global_device_ids=true | all-gather | bytes 393216 | tf_op jit(solution)/shard_map/all_gather | solution.py:222
  148.6 2.6 %shard_map.82 = (f32[256,128]{1,0:T(8,128)S(1)}, f32[256,128]{1,0:T(8,128)S(1)}, f32[256,128]{1,0:T(8,128)S(1)}, f32[256,128]{1,0:T(8,128)S(1)}) custom-call(s32[256]{0:T(256)S(1)} %copy-done.2, f32[512,128]{1,0:T(8,128)S(1)} %all_gather.18.both_ref, f32[256,128]{1,0:T(8,128)S(1)} %get-tuple-element.19.sol_in, f32[256,128]{1,0:T(8,128)S(1)} %get-tuple-element.20.res_in, ...), custom_call_target="tpu_custom_call" | custom-call | tf_op jit(solution)/shard_map/pallas_call | solution.py:168
  151.2 16.5 %all_gather.19.both_ref = f32[512,128]{1,0:T(8,128)S(1)} all-gather(f32[256,128]{1,0:T(8,128)S(1)} %get-tuple-element.22), channel_id=1, replica_groups=mesh['y'=8,'x'=4,'zl'=6,'zh'=2,'core'=2] {'zh'}, dimensions={0}, use_global_device_ids=true | all-gather | bytes 393216 | tf_op jit(solution)/shard_map/all_gather | solution.py:222
  167.7 0.8 shard_map.83
  (5 shorter events, 0.0 us)
Async XLA Ops:
  0.6 80.4 %copy-start = (bf16[512,128]{1,0:T(8,128)(2,1)S(1)}, bf16[512,128]{1,0:T(8,128)(2,1)}, u32[]{:S(2)}) copy-start(bf16[512,128]{1,0:T(8,128)(2,1)} %param.6) | copy-start | bytes 393220
  20.6 53.6 %copy-start.3 = (s32[1,1,32,128,128]{4,3,2,1,0:T(8,128)S(1)}, s32[1,1,32,128,128]{4,3,2,1,0:T(8,128)}, u32[]{:S(2)}) copy-start(s32[1,1,32,128,128]{4,3,2,1,0:T(8,128)} %param.10) | copy-start | bytes 6291460
  66.8 9.8 %copy-start.4 = (s32[1,1,32]{2,1,0:T(1,128)S(1)}, s32[1,1,32]{2,1,0:T(1,128)}, u32[]{:S(2)}) copy-start(s32[1,1,32]{2,1,0:T(1,128)} %param.9) | copy-start | bytes 388
  66.8 9.8 %copy-start.5 = (s32[1,1,32]{2,1,0:T(1,128)S(1)}, s32[1,1,32]{2,1,0:T(1,128)}, u32[]{:S(2)}) copy-start(s32[1,1,32]{2,1,0:T(1,128)} %param.8) | copy-start | bytes 388
  66.8 17.0 %collective-permute-start = (bf16[6144,128]{1,0:T(8,128)(2,1)S(1)}, bf16[6144,128]{1,0:T(8,128)(2,1)}, u32[]{:S(2)}, u32[]{:S(2)}) collective-permute-start(bf16[6144,128]{1,0:T(8,128)(2,1)S(1)} %bitcast.16), channel_id=1, source_target_pairs={{0,1},{1,0},{2,3},{3,2},{4,5},{5,4},{6,7},{7,6},{8,9},{9,8},{10,11... | collective-permute-start | bytes 4718600 | tf_op jit(solution)/shard_map/ppermute | solution.py:188
  74.6 9.2 %collective-permute-start.1 = (bf16[33,128,128]{2,1,0:T(8,128)(2,1)S(1)}, bf16[33,128,128]{2,1,0:T(8,128)(2,1)}, u32[]{:S(2)}, u32[]{:S(2)}) collective-permute-start(bf16[33,128,128]{2,1,0:T(8,128)(2,1)S(1)} %select_convert_fusion.refs_4_.m0), channel_id=1, source_target_pairs={{0,1},{1,0},{2,3},{3,2},{4,5},{5,4},{6,7},{7,6},{8,9},{9,8},{10,11... | collective-permute-start | bytes 3244040 | tf_op jit(solution)/shard_map/ppermute | solution.py:188
  83.8 0.7 copy-start.1
  84.5 25.0 %copy-start.2 = (s32[256]{0:T(256)S(1)}, s32[256]{0:T(256)}, u32[]{:S(2)}) copy-start(s32[256]{0:T(256)} %shard_map.77.refs_0_.lists_ref) | copy-start | bytes 3076

commit v2 on v1

--- a/solution.py
+++ b/solution.py
@@ -10,9 +10,10 @@
 REGULARIZE = 0.5
 EPSILON = 1e-06
 
-ROW = ("y", "x", "zl")
+ROW = ("y4", "y2", "y1", "x2", "x1", "z3", "z1")
 COL = ("zh", "core")
-SIZES = {"y": 8, "x": 4, "zl": 6, "zh": 2, "core": 2}
+SIZES = {"y4": 2, "y2": 2, "y1": 2, "x2": 2, "x1": 2, "z3": 3, "z1": 2, "zh": 2, "core": 2}
+STAGES = (("y4", "y2", "z3"), ("y1", "x2", "x1", "z1"))
 
 BLK = 128
 K = 128
@@ -58,7 +59,7 @@
 
 
 def gram_of(v_ref):
-    step = 512
+    step = 2048
 
     def body(i, total):
         block = v_ref[pl.ds(pl.multiple_of(i * step, step), step), :]
@@ -73,37 +74,53 @@
     out_ref[...] = gram_of(v_ref)
 
 
+def picked(lists_ref, v_refs, m_refs, i, r, take):
+    cols, masks = [], []
+    for g in range(2):
+        for k in range(take):
+            entry = lists_ref[(2 * g + r) * STRIDE + take * i + k]
+            start = pl.multiple_of((entry & (SHIFT - 1)) * BLK, BLK)
+            cols.append(v_refs[g][pl.ds(start, BLK), :])
+            masks.append(m_refs[g][entry >> 6])
+    return jnp.concatenate(cols, axis=0), jnp.concatenate(masks, axis=1)
+
+
+def weigh(rows, block, mask, opening):
+    scores = lax.dot_general(
+        rows, block, (((1,), (1,)), ((), ())), preferred_element_type=jnp.float32
+    )
+    if opening:
+        scores = (1.0 + CONFIDENCE) / CONFIDENCE - scores
+    return scores.astype(jnp.bfloat16) * mask
+
+
 def add_sparse(lists_ref, x_ref, v_refs, m_refs, out_ref, opening):
     def body(i, carry):
+        parts = []
         for r in range(2):
-            cols = []
-            masks = []
-            for g in range(2):
-                for k in range(2):
-                    entry = lists_ref[(2 * g + r) * STRIDE + 2 * i + k]
-                    slot = lax.div(entry, SHIFT)
-                    start = pl.multiple_of(lax.rem(entry, SHIFT) * BLK, BLK)
-                    cols.append(v_refs[g][pl.ds(start, BLK), :])
-                    masks.append(m_refs[g][slot])
-            block = jnp.concatenate(cols, axis=0)
-            mask = jnp.concatenate(masks, axis=1)
-            rows = x_ref[pl.ds(r * BLK, BLK), :]
-            scores = lax.dot_general(
-                rows, block, (((1,), (1,)), ((), ())), preferred_element_type=jnp.float32
-            )
-            if opening:
-                scores = (1.0 + CONFIDENCE) / CONFIDENCE - scores
-            weights = scores.astype(jnp.bfloat16) * mask
+            for h in range(2):
+                block, mask = picked(lists_ref, v_refs, m_refs, 2 * i + h, r, 2)
+                parts.append((r, block, weigh(x_ref[pl.ds(r * BLK, BLK), :], block, mask, opening)))
+        for r, block, weights in parts:
             out_ref[pl.ds(r * BLK, BLK), :] += jnp.dot(
                 weights, block, preferred_element_type=jnp.float32
             )
         return carry
 
-    lax.fori_loop(0, lists_ref[TRIPS], body, 0)
+    lax.fori_loop(0, lax.div(lists_ref[TRIPS] + 1, 2), body, 0)
+
+
+def halves(a):
+    high = a.astype(jnp.bfloat16)
+    return high, (a - high.astype(jnp.float32)).astype(jnp.bfloat16)
 
 
 def exact_dot(a, b):
-    return jnp.dot(a, b, precision=lax.Precision.HIGHEST, preferred_element_type=jnp.float32)
+    a_high, a_low = halves(a)
+    b_high, b_low = halves(b)
+    left = jnp.concatenate([a_high, a_high, a_low], axis=1)
+    right = jnp.concatenate([b_high, b_low, b_high], axis=0)
+    return jnp.dot(left, right, preferred_element_type=jnp.float32)
 
 
 def init_kernel(gravity, lists_ref, x_ref, v0, v1, m0, m1, own_gram, part_ref, gram_ref):
@@ -175,13 +192,20 @@
     )(*args)
 
 
-def gather_by_exchange(block, axes):
+def gather_stage(block, axes):
     count = 1
     for axis in axes:
         count *= SIZES[axis]
     sent = jnp.broadcast_to(block[None], (count,) + block.shape)
-    got = lax.all_to_all(sent, axes, 0, 0, tiled=True)
-    return got.reshape(count * block.shape[0], block.shape[1])
+    return lax.all_to_all(sent, axes, 0, 0, tiled=True).reshape(-1, block.shape[1])
+
+
+def in_order(block):
+    held = sum(reversed(STAGES), ())
+    piece = block.shape[0] // 192
+    block = block.reshape(tuple(SIZES[axis] for axis in held) + (piece, block.shape[1]))
+    order = tuple(held.index(axis) for axis in ROW) + (len(held), len(held) + 1)
+    return block.transpose(order).reshape(-1, block.shape[-1])
 
 
 def swap(value):
@@ -209,7 +233,11 @@
         out_specs=pl.BlockSpec(memory_space=pltpu.SMEM),
     )(ids)
 
-    own = gather_by_exchange(gather_by_exchange(col_factors, ("zl",)), ("y", "x"))
+    own = col_factors
+    for axes in STAGES:
+        own = gather_stage(own, axes)
+    own, lists, own_masks, other_masks = lax.optimization_barrier((own, lists, own_masks, other_masks))
+    own = in_order(own)
     other = swap(own)
     (own_gram,) = on_chip(gram_kernel, (own,), [((K, K), f32)], smem=0)
 

time: 169 us -> 136 us (0.80)
  the two profiles are of different devices: /device:TPU:9 before, /device:TPU:6 now
where the time goes in v2:
time: 136 us
  blocking collectives  90 us (66%)
  Pallas kernels  15 us (11%)
  waiting for transfers between devices  13.5 us (10%)
  starting transfers between devices  9.84 us (7%)
  local copies, waits for them, and re-layouts  5.16 us (4%)
  between operations  1.48 us (1%)
    all_gather x4, blocking collectives, both(): return lax.all_gather(part, 'zh', axis=0, tiled=True)  58.2 us
    all_to_all x1, blocking collectives, gather_stage(): lax.all_to_all(sent, axes, 0, 0, tiled=True).reshape(-1, block.shape[1])  29.2 us
    pallas_call x6, Pallas kernels, on_chip(): pl.pallas_call(kernel, out_shape=[jax.ShapeDtypeStruct(shape, dtype) for...  13.2 us
    all_to_all x1, waiting for transfers between devices, gather_stage(): lax.all_to_all(sent, axes, 0, 0, tiled=True).reshape(-1, block.shape[1])  11.1 us
    all_to_all x1, starting transfers between devices, gather_stage(): lax.all_to_all(sent, axes, 0, 0, tiled=True).reshape(-1, block.shape[1])  6 us
    ppermute x2, starting transfers between devices, swap(): return lax.ppermute(value, 'core', [(0, 1), (1, 0)])  3.84 us
  transfers between devices with their start and end apart: 3, of which 2 were waited for; matrix products, arithmetic and copies ran while one was open for 0% of the time, Pallas kernels for 2%

profile of v2, /device:TPU:6, one launch (start us, length us, event | category | flops | bytes accessed | tf_op | source)
XLA Modules:
  0.0 135.6 jit_solution(17822173094250833102)
XLA Ops:
  0.6 0.0 copy-start
  0.6 0.7 broadcast_in_dim.28
  1.4 29.2 %all_to_all.10 = bf16[12,32,128]{2,1,0:T(8,128)(2,1)S(1)} all-to-all(bf16[12,32,128]{2,1,0:T(8,128)(2,1)S(1)} %broadcast_in_dim.28), channel_id=1, replica_groups=mesh['y4'=2,'y2'=2,'y1'=2,'x2'=2,'x1'=2,'z3'=3,'z1'=2,'zh'=2,'core'=2] {..., dimensions={0} | all-to-all | bytes 196608 | tf_op jit(solution)/shard_map/all_to_all | solution.py:200
  30.6 1.4 %broadcast_in_dim.30 = bf16[16,384,128]{2,1,0:T(8,128)(2,1)} broadcast(bf16[384,128]{1,0:T(8,128)(2,1)S(1)} %bitcast.30), dimensions={1,2} | broadcast | bytes 1671168 | tf_op jit(solution)/shard_map/broadcast_in_dim | solution.py:199
  32.0 6.0 %all-to-all-start.1 = ((bf16[16,384,128]{2,1,0:T(8,128)(2,1)}), bf16[16,384,128]{2,1,0:T(8,128)(2,1)}, u32[]{:S(2)}, u32[]{:S(2)}) async-start(bf16[16,384,128]{2,1,0:T(8,128)(2,1)} %broadcast_in_dim.30), calls=%async_computation.1 | async-start | bytes 3145728 | tf_op jit(solution)/shard_map/all_to_all | solution.py:200
  38.1 0.0 copy-start.6
  38.7 0.0 copy-done.4
  38.8 0.5 select_convert_fusion.refs_4_.m0
  39.2 1.9 %collective-permute-start = (bf16[33,128,128]{2,1,0:T(8,128)(2,1)S(1)}, bf16[33,128,128]{2,1,0:T(8,128)(2,1)S(1)}, u32[]{:S(2)}, u32[]{:S(2)}) collective-permute-start(bf16[33,128,128]{2,1,0:T(8,128)(2,1)S(1)} %select_convert_fusion.refs_4_.m0), channel_id=1, source_target_pairs={{0,1},{1,0},{2,3},{3,2},{4,5},{5,4},{6,7},{7,6},{8,9},{9,8},{10,11... | collective-permute-start | bytes 3244040 | tf_op jit(solution)/shard_map/ppermute | solution.py:212
  41.2 0.0 copy-done.5
  41.2 0.0 copy-done.6
  41.2 0.1 add_bitcast_fusion
  41.3 2.7 %all-gather.1 = s32[2,1,128]{2,1,0:T(1,128)} all-gather(s32[1,1,128]{2,1,0:T(1,128)S(1)} %add_bitcast_fusion), channel_id=2, replica_groups=mesh['y4'=2,'y2'=2,'y1'=2,'x2'=2,'x1'=2,'z3'=3,'z1'=2,'zh'=2,'core'=2] {..., dimensions={0}, use_global_device_ids=true | all-gather | bytes 1536 | tf_op jit(solution)/shard_map/all_gather | solution.py:228
  43.9 1.8 %shard_map.77.refs_0_.lists_ref = s32[256]{0:T(256)} custom-call(s32[2,128]{1,0:T(2,128)} %bitcast.31), custom_call_target="tpu_custom_call" | custom-call | tf_op jit(solution)/shard_map/pallas_call | solution.py:229
  45.7 0.0 collective-permute-done.refs_5_.m1
  45.7 0.0 copy-start.1
  45.7 1.0 copy-done.1
  46.8 11.1 %all-to-all-done.1 = bf16[16,384,128]{2,1,0:T(8,128)(2,1)} async-done(((bf16[16,384,128]{2,1,0:T(8,128)(2,1)}), bf16[16,384,128]{2,1,0:T(8,128)(2,1)}, u32[]{:S(2)}, u32[]{:S(2)}) %all-to-all-start.1) | async-done | bytes 1572896 | tf_op jit(solution)/shard_map/all_to_all | solution.py:200
  57.9 1.9 %copy.14 = bf16[2,2,2,2,2,3,2,32,128]{8,7,6,5,4,3,2,1,0:T(8,128)(2,1)S(1)} copy(bf16[2,2,2,2,2,3,2,32,128]{8,7,5,1,0,6,4,3,2:T(8,128)(2,1)} %bitcast.11) | data formatting | bytes 3145728 | tf_op jit(solution)/shard_map/transpose | solution.py:208
  59.8 1.9 %collective-permute-start.1 = (bf16[6144,128]{1,0:T(8,128)(2,1)S(1)}, bf16[6144,128]{1,0:T(8,128)(2,1)}, u32[]{:S(2)}, u32[]{:S(2)}) collective-permute-start(bf16[6144,128]{1,0:T(8,128)(2,1)S(1)} %bitcast.20), channel_id=1, source_target_pairs={{0,1},{1,0},{2,3},{3,2},{4,5},{5,4},{6,7},{7,6},{8,9},{9,8},{10,11... | collective-permute-start | bytes 4718600 | tf_op jit(solution)/shard_map/ppermute | solution.py:212
  61.7 0.0 copy-done
  61.8 1.0 shard_map.78.refs_6_
  62.8 2.4 %collective-permute-done.1.refs_3_.v1 = bf16[6144,128]{1,0:T(8,128)(2,1)} collective-permute-done((bf16[6144,128]{1,0:T(8,128)(2,1)S(1)}, bf16[6144,128]{1,0:T(8,128)(2,1)}, u32[]{:S(2)}, u32[]{:S(2)}) %collective-permute-start.1) | collective-permute-done | bytes 1572896 | tf_op jit(solution)/shard_map/ppermute | solution.py:212
  65.2 3.5 %shard_map.79 = (f32[256,128]{1,0:T(8,128)S(1)}, f32[128,128]{1,0:T(8,128)S(1)}) custom-call(s32[256]{0:T(256)S(1)} %copy-done.3, bf16[256,128]{1,0:T(8,128)(2,1)S(1)} %bitcast.26, bf16[6144,128]{1,0:T(8,128)(2,1)S(1)} %bitcast.22, bf16[6144,128]{1,0:T(8,128)(2,1)} %collective-permute-done.1.refs_3_.v1, ...), custom_call_target="tpu_custom_call" | custom-call | tf_op jit(solution)/shard_map/pallas_call | solution.py:185
  68.8 13.2 %all_gather.16.both_ref = f32[512,128]{1,0:T(8,128)S(1)} all-gather(f32[256,128]{1,0:T(8,128)S(1)} %get-tuple-element.22), channel_id=1, replica_groups=mesh['y4'=2,'y2'=2,'y1'=2,'x2'=2,'x1'=2,'z3'=3,'z1'=2,'zh'=2,'core'=2] {..., dimensions={0}, use_global_device_ids=true | all-gather | bytes 393216 | tf_op jit(solution)/shard_map/all_gather | solution.py:250
  82.0 2.5 %shard_map.80 = (f32[256,128]{1,0:T(8,128)S(1)}, f32[256,128]{1,0:T(8,128)S(1)}) custom-call(s32[256]{0:T(256)S(1)} %copy-done.3, f32[512,128]{1,0:T(8,128)S(1)} %all_gather.16.both_ref, bf16[256,128]{1,0:T(8,128)(2,1)S(1)} %bitcast.27, bf16[6144,128]{1,0:T(8,128)(2,1)S(1)} %bitcast.23, bf16[6144,128]{1,0:T(8,128)(2,1)} %collective-permute-done.1.refs_3_.v1, ...), custom_call_target="tpu_custom_call" | custom-call | tf_op jit(solution)/shard_map/pallas_call | solution.py:185
  84.5 15.9 %all_gather.17.both_ref = f32[512,128]{1,0:T(8,128)S(1)} all-gather(f32[256,128]{1,0:T(8,128)S(1)} %get-tuple-element.24), channel_id=1, replica_groups=mesh['y4'=2,'y2'=2,'y1'=2,'x2'=2,'x1'=2,'z3'=3,'z1'=2,'zh'=2,'core'=2] {..., dimensions={0}, use_global_device_ids=true | all-gather | bytes 393216 | tf_op jit(solution)/shard_map/all_gather | solution.py:250
  100.4 2.7 %shard_map.81 = (f32[256,128]{1,0:T(8,128)S(1)}, f32[256,128]{1,0:T(8,128)S(1)}, f32[256,128]{1,0:T(8,128)S(1)}, f32[256,128]{1,0:T(8,128)S(1)}) custom-call(s32[256]{0:T(256)S(1)} %copy-done.3, f32[512,128]{1,0:T(8,128)S(1)} %all_gather.17.both_ref, bf16[256,128]{1,0:T(8,128)(2,1)S(1)} %bitcast.28, f32[256,128]{1,0:T(8,128)S(1)} %get-tuple-element.25.res_in.dir_in, ...), custom_call_target="tpu_custom_call" | custom-call | tf_op jit(solution)/shard_map/pallas_call | solution.py:185
  103.1 15.7 %all_gather.18.both_ref = f32[512,128]{1,0:T(8,128)S(1)} all-gather(f32[256,128]{1,0:T(8,128)S(1)} %get-tuple-element.26), channel_id=1, replica_groups=mesh['y4'=2,'y2'=2,'y1'=2,'x2'=2,'x1'=2,'z3'=3,'z1'=2,'zh'=2,'core'=2] {..., dimensions={0}, use_global_device_ids=true | all-gather | bytes 393216 | tf_op jit(solution)/shard_map/all_gather | solution.py:250
  118.8 2.7 %shard_map.82 = (f32[256,128]{1,0:T(8,128)S(1)}, f32[256,128]{1,0:T(8,128)S(1)}, f32[256,128]{1,0:T(8,128)S(1)}, f32[256,128]{1,0:T(8,128)S(1)}) custom-call(s32[256]{0:T(256)S(1)} %copy-done.3, f32[512,128]{1,0:T(8,128)S(1)} %all_gather.18.both_ref, f32[256,128]{1,0:T(8,128)S(1)} %get-tuple-element.27.sol_in, f32[256,128]{1,0:T(8,128)S(1)} %get-tuple-element.28.res_in, ...), custom_call_target="tpu_custom_call" | custom-call | tf_op jit(solution)/shard_map/pallas_call | solution.py:185
  121.5 13.3 %all_gather.19.both_ref = f32[512,128]{1,0:T(8,128)S(1)} all-gather(f32[256,128]{1,0:T(8,128)S(1)} %get-tuple-element.30), channel_id=1, replica_groups=mesh['y4'=2,'y2'=2,'y1'=2,'x2'=2,'x1'=2,'z3'=3,'z1'=2,'zh'=2,'core'=2] {..., dimensions={0}, use_global_device_ids=true | all-gather | bytes 393216 | tf_op jit(solution)/shard_map/all_gather | solution.py:250
  134.8 0.8 shard_map.83
  (9 shorter events, 0.0 us)
Async XLA Ops:
  0.6 61.1 %copy-start = (bf16[512,128]{1,0:T(8,128)(2,1)S(1)}, bf16[512,128]{1,0:T(8,128)(2,1)}, u32[]{:S(2)}) copy-start(bf16[512,128]{1,0:T(8,128)(2,1)} %param.6) | copy-start | bytes 393220
  30.6 8.1 %copy-start.4 = (s32[1,1,32,128,128]{4,3,2,1,0:T(8,128)S(1)}, s32[1,1,32,128,128]{4,3,2,1,0:T(8,128)}, u32[]{:S(2)}) copy-start(s32[1,1,32,128,128]{4,3,2,1,0:T(8,128)} %param.10) | copy-start | bytes 6291460
  32.0 25.8 %all-to-all-start.1 = ((bf16[16,384,128]{2,1,0:T(8,128)(2,1)}), bf16[16,384,128]{2,1,0:T(8,128)(2,1)}, u32[]{:S(2)}, u32[]{:S(2)}) async-start(bf16[16,384,128]{2,1,0:T(8,128)(2,1)} %broadcast_in_dim.30), calls=%async_computation.1 | async-start | bytes 3145728 | tf_op jit(solution)/shard_map/all_to_all | solution.py:200
  38.1 3.1 %copy-start.5 = (s32[1,1,32]{2,1,0:T(1,128)S(1)}, s32[1,1,32]{2,1,0:T(1,128)}, u32[]{:S(2)}) copy-start(s32[1,1,32]{2,1,0:T(1,128)} %param.9) | copy-start | bytes 388
  38.1 3.1 %copy-start.6 = (s32[1,1,32]{2,1,0:T(1,128)S(1)}, s32[1,1,32]{2,1,0:T(1,128)}, u32[]{:S(2)}) copy-start(s32[1,1,32]{2,1,0:T(1,128)} %param.8) | copy-start | bytes 388
  39.2 6.5 %collective-permute-start = (bf16[33,128,128]{2,1,0:T(8,128)(2,1)S(1)}, bf16[33,128,128]{2,1,0:T(8,128)(2,1)S(1)}, u32[]{:S(2)}, u32[]{:S(2)}) collective-permute-start(bf16[33,128,128]{2,1,0:T(8,128)(2,1)S(1)} %select_convert_fusion.refs_4_.m0), channel_id=1, source_target_pairs={{0,1},{1,0},{2,3},{3,2},{4,5},{5,4},{6,7},{7,6},{8,9},{9,8},{10,11... | collective-permute-start | bytes 3244040 | tf_op jit(solution)/shard_map/ppermute | solution.py:212
  45.7 1.0 copy-start.1
  57.9 7.4 %copy-start.3 = (s32[256]{0:T(256)S(1)}, s32[256]{0:T(256)}, u32[]{:S(2)}) copy-start(s32[256]{0:T(256)} %shard_map.77.refs_0_.lists_ref) | copy-start | bytes 3076
  59.8 5.4 %collective-permute-start.1 = (bf16[6144,128]{1,0:T(8,128)(2,1)S(1)}, bf16[6144,128]{1,0:T(8,128)(2,1)}, u32[]{:S(2)}, u32[]{:S(2)}) collective-permute-start(bf16[6144,128]{1,0:T(8,128)(2,1)S(1)} %bitcast.20), channel_id=1, source_target_pairs={{0,1},{1,0},{2,3},{3,2},{4,5},{5,4},{6,7},{7,6},{8,9},{9,8},{10,11... | collective-permute-start | bytes 4718600 | tf_op jit(solution)/shard_map/ppermute | solution.py:212
  61.7 3.5 %copy-start.2 = (bf16[33,128,128]{2,1,0:T(8,128)(2,1)S(1)}, bf16[33,128,128]{2,1,0:T(8,128)(2,1)}, u32[]{:S(2)}) copy-start(bf16[33,128,128]{2,1,0:T(8,128)(2,1)} %copy-done.1) | copy-start | bytes 3244036

commit v3 on v2

v3 whole, which is shorter than its diff:
```python
import jax
import jax.numpy as jnp
from jax import lax
from jax.experimental import pallas as pl
from jax.experimental.pallas import tpu as pltpu
from jax.sharding import Mesh, PartitionSpec as P

ITERS = 3
CONFIDENCE = 2.0
REGULARIZE = 0.5
EPSILON = 1e-06

ROW = ("y4", "y2", "y1", "x2", "x1", "z3", "z1")
COL = ("zh", "core")
SIZES = {"y4": 2, "y2": 2, "y1": 2, "x2": 2, "x1": 2, "z3": 3, "z1": 2, "zh": 2, "core": 2}
STAGES = (("zh", "z3", "z1"), ("y4", "y2"), ("y1", "x2", "x1"))

BLK = 128
K = 128
NB = 32
PIECE = 2 * BLK
STRIDE = NB
TRIPS = 4 * STRIDE
HALF = BLK // 2
SHIFT = 256
VMEM_LIMIT = 40 * 1024 * 1024


def lists_kernel(own_ref, other_ref, out_ref):
    half = lax.axis_index("zh")

    def clear(i, carry):
        out_ref[i] = NB * SHIFT * SHIFT
        return carry

    lax.fori_loop(0, 4 * STRIDE, clear, 0, unroll=8)
    longest = jnp.int32(0)
    for group, ids_ref in enumerate((own_ref, other_ref)):
        side = half if group == 0 else 1 - half

        def place(slot, ends, ids_ref=ids_ref, group=group, side=side):
            low, high = ends
            row = ids_ref[slot]
            entry = slot
            for k in range(2):
                piece = 2 * ids_ref[NB + slot] + k
                chip = lax.div(piece, 3)
                y, x = chip >> 2, chip & 3
                spot = ((((y & 1) * 4 + x) * 4 + (y >> 1)) * 2 + side) * 3 + lax.rem(piece, 3)
                entry = entry * SHIFT + spot
            mine = (row >> 1) == half
            upper = (row & 1) == 1

            @pl.when(mine)
            def _():
                out_ref[jnp.where(upper, (2 * group + 1) * STRIDE + high, 2 * group * STRIDE + low)] = entry

            low = low + jnp.where(mine & jnp.logical_not(upper), 1, 0)
            high = high + jnp.where(mine & upper, 1, 0)
            return low, high

        low, high = lax.fori_loop(0, ids_ref[2 * NB], place, (jnp.int32(0), jnp.int32(0)))
        longest = jnp.maximum(longest, jnp.maximum(low, high))
    out_ref[TRIPS] = lax.div(longest + 1, 2)


def gram_of(v_ref):
    step = 2048

    def body(i, total):
        block = v_ref[pl.ds(pl.multiple_of(i * step, step), step), :]
        return total + lax.dot_general(
            block, block, (((0,), (0,)), ((), ())), preferred_element_type=jnp.float32
        )

    return lax.fori_loop(0, v_ref.shape[0] // step, body, jnp.zeros((K, K), jnp.float32))


def picked(lists_ref, v_ref, m_refs, groups, i, r, take):
    cols, masks = [], []
    for g in groups:
        for k in range(take):
            entry = lists_ref[(2 * g + r) * STRIDE + take * i + k]
            for spot in (lax.div(entry, SHIFT) & (SHIFT - 1), entry & (SHIFT - 1)):
                cols.append(v_ref[pl.ds(pl.multiple_of(spot * HALF, HALF), HALF), :])
            slot = lax.div(entry, SHIFT * SHIFT)
            mask = m_refs[g][slot & (NB - 1)]
            masks.append(jnp.where(slot < NB, mask, jnp.zeros_like(mask)))
    return jnp.concatenate(cols, axis=0), jnp.concatenate(masks, axis=1)


def weigh(rows, block, mask, opening):
    scores = lax.dot_general(
        rows, block, (((1,), (1,)), ((), ())), preferred_element_type=jnp.float32
    )
    if opening:
        scores = (1.0 + CONFIDENCE) / CONFIDENCE - scores
    return scores.astype(jnp.bfloat16) * mask


def add_sparse(lists_ref, x_ref, v_ref, m_refs, out_ref, opening, groups=(0, 1)):
    def body(i, carry):
        parts = []
        for r in range(2):
            for h in range(2):
                block, mask = picked(lists_ref, v_ref, m_refs, groups, 2 * i + h, r, 2)
                parts.append((r, block, weigh(x_ref[pl.ds(r * BLK, BLK), :], block, mask, opening)))
        for r, block, weights in parts:
            out_ref[pl.ds(r * BLK, BLK), :] += jnp.dot(
                weights, block, preferred_element_type=jnp.float32
            )
        return carry

    lax.fori_loop(0, lax.div(lists_ref[TRIPS] + 1, 2), body, 0)


def halves(a):
    high = a.astype(jnp.bfloat16)
    return high, (a - high.astype(jnp.float32)).astype(jnp.bfloat16)


def exact_dot(a, b):
    a_high, a_low = halves(a)
    b_high, b_low = halves(b)
    left = jnp.concatenate([a_high, a_high, a_low], axis=1)
    right = jnp.concatenate([b_high, b_low, b_high], axis=0)
    return jnp.dot(left, right, preferred_element_type=jnp.float32)


def early_kernel(gravity, lists_ref, x_ref, v_in, m0, v_ref, gram_ref, part_ref):
    v_ref[...] = v_in[...]
    gram = gravity * gram_of(v_in)
    gram_ref[...] = gram
    part_ref[...] = -exact_dot(x_ref[...].astype(jnp.float32), gram)
    add_sparse(lists_ref, x_ref, v_in, (m0, None), part_ref, True, (0,))


def init_kernel(lists_ref, x_ref, v_ref, m1, part_in, part_ref):
    part_ref[...] = part_in[...]
    add_sparse(lists_ref, x_ref, v_ref, (None, m1), part_ref, True, (1,))


def row_sum(a):
    return jnp.sum(a, axis=1, keepdims=True)


def advance(both, direction, residual, sol):
    image = both + REGULARIZE * direction
    norm_now = row_sum(residual * residual)
    step = norm_now / (row_sum(direction * image) + EPSILON)
    sol = sol + step * direction
    residual = residual - step * image
    return sol, residual, norm_now


def image_part(lists_ref, d, low_ref, v_ref, m0, m1, gram_ref, part_ref):
    low_ref[...] = d.astype(jnp.bfloat16)
    part_ref[...] = exact_dot(d, gram_ref[...])
    add_sparse(lists_ref, low_ref, v_ref, (m0, m1), part_ref, False)


def start_kernel(lists_ref, both_ref, x_ref, v_ref, m0, m1, gram_ref, res_ref, part_ref, low_ref):
    residual = both_ref[:PIECE] + both_ref[PIECE:] - REGULARIZE * x_ref[...].astype(jnp.float32)
    res_ref[...] = residual
    image_part(lists_ref, residual, low_ref, v_ref, m0, m1, gram_ref, part_ref)


def step_kernel(
    lists_ref, both_ref, sol_in, res_in, dir_in, v_ref, m0, m1, gram_ref,
    sol_ref, res_ref, dir_ref, part_ref, low_ref,
):
    direction = dir_in[...]
    sol, residual, norm_now = advance(
        both_ref[:PIECE] + both_ref[PIECE:], direction, res_in[...], sol_in[...].astype(jnp.float32)
    )
    sol_ref[...] = sol
    res_ref[...] = residual
    direction = residual + row_sum(residual * residual) / (norm_now + EPSILON) * direction
    dir_ref[...] = direction
    image_part(lists_ref, direction, low_ref, v_ref, m0, m1, gram_ref, part_ref)


def last_kernel(both_ref, sol_in, res_in, dir_in, sol_ref, res_ref):
    start = pl.multiple_of(lax.axis_index("core") * BLK, BLK)
    mine = pl.ds(start, BLK)
    both = both_ref[mine, :] + both_ref[pl.ds(start + PIECE, BLK), :]
    sol, residual, _ = advance(both, dir_in[mine, :], res_in[mine, :], sol_in[mine, :])
    sol_ref[...] = sol.astype(jnp.bfloat16)
    res_ref[...] = residual


def on_chip(kernel, args, outs, scratch=(), smem=1):
    vmem = pl.BlockSpec(memory_space=pltpu.VMEM)
    scalar = pl.BlockSpec(memory_space=pltpu.SMEM)
    return pl.pallas_call(
        kernel,
        out_shape=[jax.ShapeDtypeStruct(shape, dtype) for shape, dtype in outs],
        in_specs=[scalar] * smem + [vmem] * (len(args) - smem),
        out_specs=[vmem] * len(outs),
        scratch_shapes=list(scratch),
        compiler_params=pltpu.CompilerParams(vmem_limit_bytes=VMEM_LIMIT),
    )(*args)


def made_lists(ids, others):
    return pl.pallas_call(
        lists_kernel,
        out_shape=jax.ShapeDtypeStruct((2 * TRIPS,), jnp.int32),
        in_specs=[pl.BlockSpec(memory_space=pltpu.SMEM)] * 2,
        out_specs=pl.BlockSpec(memory_space=pltpu.SMEM),
    )(ids, others)


def gather_stage(block, axes):
    count = 1
    for axis in axes:
        count *= SIZES[axis]
    sent = jnp.broadcast_to(block[None], (count,) + block.shape)
    return lax.all_to_all(sent, axes, 0, 0, tiled=True).reshape(-1, block.shape[1])


def swap(value):
    return lax.ppermute(value, "zh", [(0, 1), (1, 0)])


def per_device(start_rows, col_factors, block_rows, block_cols, block_masks, block_counts):
    f32, bf16 = jnp.float32, jnp.bfloat16
    half = lax.axis_index("zh")
    gravity = K / (col_factors.shape[0] * 768)

    live = (jnp.arange(NB) < block_counts[0, 0])[:, None, None]
    own_masks = jnp.where(live & (block_masks[0, 0] > 0), CONFIDENCE, 0.0).astype(bf16)
    ids = jnp.concatenate(
        [block_rows[0, 0], block_cols[0, 0], jnp.broadcast_to(block_counts[0, 0], (2 * NB,))]
    )
    extra = jnp.broadcast_to(ids.astype(bf16)[None], (16, K))
    pieces = gather_stage(jnp.concatenate([col_factors, extra]), STAGES[0])
    pieces, own_masks = lax.optimization_barrier((pieces, own_masks))
    other_masks = swap(own_masks)
    pieces = pieces.reshape(12, 48, K)
    member = (1 - half) * 6 + lax.axis_index(("z3", "z1"))
    other_ids = lax.dynamic_index_in_dim(pieces[:, 32], member, 0, keepdims=False).astype(jnp.int32)
    pieces = pieces[:, :32].reshape(12 * 32, K)

    def gathered(pieces, ids, other_ids):
        lists = made_lists(ids, other_ids)
        for axes in STAGES[1:]:
            pieces = gather_stage(pieces, axes)
        return pieces, lists

    def nothing(pieces, ids, other_ids):
        return jnp.zeros((32 * pieces.shape[0], K), bf16), jnp.zeros((2 * TRIPS,), jnp.int32)

    rows_all, lists = lax.cond(block_counts[0, 0] > 0, gathered, nothing, pieces, ids, other_ids)
    rows = lax.dynamic_slice_in_dim(start_rows, half * PIECE, PIECE, 0)
    rows_all, gram, part = on_chip(
        lambda *refs: early_kernel(gravity, *refs), (lists, rows, rows_all, own_masks),
        [(rows_all.shape, bf16), ((K, K), f32), ((PIECE, K), f32)],
    )
    big = (rows_all, own_masks, other_masks, gram)
    whole = ((PIECE, K), f32)
    low = (pltpu.VMEM((PIECE, K), bf16),)

    def both(part):
        return lax.all_gather(part, "core", axis=0, tiled=True)

    (part,) = on_chip(init_kernel, (lists, rows, rows_all, other_masks, part), [whole])
    residual, part = on_chip(start_kernel, (lists, both(part), rows) + big, [whole] * 2, low)
    sol, direction = rows, residual
    for _ in range(ITERS - 1):
        sol, residual, direction, part = on_chip(
            step_kernel, (lists, both(part), sol, residual, direction) + big, [whole] * 4, low
        )
    return tuple(
        on_chip(
            last_kernel, (both(part), sol, residual, direction), [((BLK, K), bf16), ((BLK, K), f32)], smem=0
        )
    )


def solution(mesh):
    fine = Mesh(mesh.devices.reshape(tuple(SIZES.values())), tuple(SIZES))
    placed = (
        P(ROW, None),
        P(ROW + COL, None),
        P(ROW, COL, None),
        P(ROW, COL, None),
        P(ROW, COL, None, None, None),
        P(ROW, COL),
    )
    return jax.shard_map(
        per_device,
        mesh=fine,
        in_specs=placed,
        out_specs=(P(ROW + COL, None), P(ROW + COL, None)),
        check_vma=False,
    )
```

time: 136 us -> 127 us (0.934)
  the two profiles are of different devices: /device:TPU:6 before, /device:TPU:61 now
where the time goes in v3:
time: 127 us
  waiting for transfers between devices  50.9 us (40%)
  starting transfers between devices  27.4 us (22%)
  blocking collectives  21.2 us (17%)
  Pallas kernels  18.9 us (15%)
  other arithmetic  4.04 us (3%)
  local copies, waits for them, and re-layouts  2.81 us (2%)
  between operations  1.43 us (1%)
    all_to_all x2, waiting for transfers between devices, gather_stage(): lax.all_to_all(sent, axes, 0, 0, tiled=True).reshape(-1, block.shape[1])  42 us
    all_to_all x2, starting transfers between devices, gather_stage(): lax.all_to_all(sent, axes, 0, 0, tiled=True).reshape(-1, block.shape[1])  23.1 us
    pallas_call x6, Pallas kernels, on_chip(): pl.pallas_call(kernel, out_shape=[jax.ShapeDtypeStruct(shape, dtype) for...  16.7 us
    all_to_all x1, blocking collectives, gather_stage(): lax.all_to_all(sent, axes, 0, 0, tiled=True).reshape(-1, block.shape[1])  13.2 us
    ppermute x1, waiting for transfers between devices, swap(): return lax.ppermute(value, 'zh', [(0, 1), (1, 0)])  8.9 us
    all_gather x4, blocking collectives, both(): return lax.all_gather(part, 'core', axis=0, tiled=True)  7.98 us
    ppermute x1, starting transfers between devices, swap(): return lax.ppermute(value, 'zh', [(0, 1), (1, 0)])  4.31 us
    broadcast_in_dim x3, local copies, waits for them, and re-layouts, gather_stage(): sent = jnp.broadcast_to(block[None], (count,) + block.shape)  2.76 us
  transfers between devices with their start and end apart: 3, of which 3 were waited for; matrix products, arithmetic and copies ran while one was open for 4% of the time, Pallas kernels for 6%

profile of v3, /device:TPU:61, one launch (start us, length us, event | category | flops | bytes accessed | tf_op | source)
XLA Modules:
  0.0 126.7 jit_solution(10589768218965435063)
XLA Ops:
  0.6 0.0 copy-start
  1.3 0.8 fusion
  2.1 0.7 pad_maximum_fusion
  2.8 0.7 broadcast_in_dim.40
  3.5 14.9 %all-to-all-start.2 = ((bf16[12,48,128]{2,1,0:T(8,128)(2,1)}), bf16[12,48,128]{2,1,0:T(8,128)(2,1)S(1)}, u32[]{:S(2)}, u32[]{:S(2)}) async-start(bf16[12,48,128]{2,1,0:T(8,128)(2,1)} %broadcast_in_dim.40), calls=%async_computation.2 | async-start | bytes 294912 | tf_op jit(solution)/shard_map/all_to_all | solution.py:219
  18.4 2.1 %select_convert_fusion.refs_3_.m0 = bf16[32,128,128]{2,1,0:T(8,128)(2,1)S(1)} fusion(s32[1,1,32,128,128]{4,3,2,1,0:T(8,128)} %param.12, pred[32]{0:T(512)(128)(4,1)S(1)} %iota_compare_fusion), kind=kLoop, calls=%fused_computation.1 | loop fusion | flops 2097152 | bytes 3145760 | tf_op jit(solution)/shard_map/convert_element_type | solution.py:232
  20.4 9.3 %all-to-all-done.2 = bf16[12,48,128]{2,1,0:T(8,128)(2,1)S(1)} async-done(((bf16[12,48,128]{2,1,0:T(8,128)(2,1)}), bf16[12,48,128]{2,1,0:T(8,128)(2,1)S(1)}, u32[]{:S(2)}, u32[]{:S(2)}) %all-to-all-start.2) | async-done | bytes 147488 | tf_op jit(solution)/shard_map/all_to_all | solution.py:219
  29.7 4.3 %collective-permute-start = (bf16[32,128,128]{2,1,0:T(8,128)(2,1)S(1)}, bf16[32,128,128]{2,1,0:T(8,128)(2,1)S(1)}, u32[]{:S(2)}, u32[]{:S(2)}) collective-permute-start(bf16[32,128,128]{2,1,0:T(8,128)(2,1)S(1)} %select_convert_fusion.refs_3_.m0), channel_id=1, source_target_pairs={{0,2},{2,0},{1,3},{3,1},{4,6},{6,4},{5,7},{7,5},{8,10},{10,8},{9,1... | collective-permute-start | bytes 3145736 | tf_op jit(solution)/shard_map/ppermute | solution.py:223
  34.0 0.0 copy-done
  34.1 59.0 %conditional.1 = (bf16[12288,128]{1,0:T(8,128)(2,1)}, s32[256]{0:T(256)S(1)}) conditional(s32[]{:T(128)} %convert_element_type.20, () %tuple.26, (bf16[576,128]{1,0:T(8,128)(2,1)S(1)}, s32[]{:T(128)}, s32[]{:T(128)}, s32[]{:T(128)}, s32[128]{0:T(128)S(1)}) %tuple.32), branch_computations={%region_0.1_spmd, %region_1.2_spmd} | conditional | flops 136 | bytes 14457746 | solution.py:254
  34.1 0.1 broadcast_in_dim.5
  34.2 13.2 %all_to_all.13 = bf16[4,384,128]{2,1,0:T(8,128)(2,1)S(1)} all-to-all(bf16[4,384,128]{2,1,0:T(8,128)(2,1)S(1)} %broadcast_in_dim.5), channel_id=1, replica_groups=mesh['y4'=2,'y2'=2,'y1'=2,'x2'=2,'x1'=2,'z3'=3,'z1'=2,'zh'=2,'core'=2] {..., dimensions={0} | all-to-all | bytes 786432 | tf_op jit(solution)/shard_map/cond/branch_1_fun/all_to_all | solution.py:219
  47.4 2.0 %broadcast_in_dim.7 = bf16[8,1536,128]{2,1,0:T(8,128)(2,1)} broadcast(bf16[1536,128]{1,0:T(8,128)(2,1)S(1)} %bitcast.18), dimensions={1,2} | broadcast | bytes 3538944 | tf_op jit(solution)/shard_map/cond/branch_1_fun/broadcast_in_dim | solution.py:218
  49.4 8.2 %all-to-all-start.1 = ((bf16[8,1536,128]{2,1,0:T(8,128)(2,1)}), bf16[8,1536,128]{2,1,0:T(8,128)(2,1)}, u32[]{:S(2)}, u32[]{:S(2)}) async-start(bf16[8,1536,128]{2,1,0:T(8,128)(2,1)} %broadcast_in_dim.7), calls=%async_computation.1 | async-start | bytes 6291456 | tf_op jit(solution)/shard_map/cond/branch_1_fun/all_to_all | solution.py:219
  57.7 0.5 bitcast_convert_fusion.other_ref
  58.2 2.2 %branch_1_fun.1 = s32[256]{0:T(256)S(1)} custom-call(s32[128]{0:T(128)S(1)} %get-tuple-element.34.own_ref, s32[128]{0:T(128)} %bitcast_convert_fusion.other_ref), custom_call_target="tpu_custom_call" | custom-call | tf_op jit(solution)/shard_map/cond/branch_1_fun/pallas_call | solution.py:206
  60.4 32.7 %all-to-all-done.1 = bf16[8,1536,128]{2,1,0:T(8,128)(2,1)} async-done(((bf16[8,1536,128]{2,1,0:T(8,128)(2,1)}), bf16[8,1536,128]{2,1,0:T(8,128)(2,1)}, u32[]{:S(2)}, u32[]{:S(2)}) %all-to-all-start.1) | async-done | bytes 3145760 | tf_op jit(solution)/shard_map/cond/branch_1_fun/all_to_all | solution.py:219
  93.1 5.9 %shard_map.77 = (bf16[12288,128]{1,0:T(8,128)(2,1)S(1)}, f32[128,128]{1,0:T(8,128)S(1)}, f32[256,128]{1,0:T(8,128)S(1)}) custom-call(s32[256]{0:T(256)S(1)} %get-tuple-element.58.refs_0_.lists_ref, bf16[256,128]{1,0:T(8,128)(2,1)S(1)} %constant_dynamic-slice_fusion.refs_1_.x_ref.sol_in, bf16[12288,128]{1,0:T(8,128)(2,1)} %get-tuple-element.59.refs_2_, ...), custom_call_target="tpu_custom_call" | custom-call | tf_op jit(solution)/shard_map/pallas_call | solution.py:195
  98.9 8.9 %collective-permute-done.m1 = bf16[32,128,128]{2,1,0:T(8,128)(2,1)S(1)} collective-permute-done((bf16[32,128,128]{2,1,0:T(8,128)(2,1)S(1)}, bf16[32,128,128]{2,1,0:T(8,128)(2,1)S(1)}, u32[]{:S(2)}, u32[]{:S(2)}) %collective-permute-start) | collective-permute-done | bytes 1048608 | tf_op jit(solution)/shard_map/ppermute | solution.py:223
  107.9 2.1 %shard_map.78 = f32[256,128]{1,0:T(8,128)S(1)} custom-call(s32[256]{0:T(256)S(1)} %get-tuple-element.58.refs_0_.lists_ref, bf16[256,128]{1,0:T(8,128)(2,1)S(1)} %constant_dynamic-slice_fusion.refs_1_.x_ref.sol_in, bf16[12288,128]{1,0:T(8,128)(2,1)S(1)} %get-tuple-element.61.v_ref, bf16[32,128,128]{2,1,0:T(8,128)(2,1)S(1)} %collective-permute-done.m1, ...), custom_call_target="tpu_custom_call" | custom-call | tf_op jit(solution)/shard_map/pallas_call | solution.py:195
  109.9 2.0 %all_gather.12.both_ref = f32[512,128]{1,0:T(8,128)S(1)} all-gather(f32[256,128]{1,0:T(8,128)S(1)} %shard_map.78), channel_id=1, replica_groups=mesh['y4'=2,'y2'=2,'y1'=2,'x2'=2,'x1'=2,'z3'=3,'z1'=2,'zh'=2,'core'=2] {..., dimensions={0}, use_global_device_ids=true | all-gather | bytes 393216 | tf_op jit(solution)/shard_map/all_gather | solution.py:265
  111.9 2.6 %shard_map.79 = (f32[256,128]{1,0:T(8,128)S(1)}, f32[256,128]{1,0:T(8,128)S(1)}) custom-call(s32[256]{0:T(256)S(1)} %get-tuple-element.58.refs_0_.lists_ref, f32[512,128]{1,0:T(8,128)S(1)} %all_gather.12.both_ref, bf16[256,128]{1,0:T(8,128)(2,1)S(1)} %constant_dynamic-slice_fusion.refs_1_.x_ref.sol_in, bf16[12288,128]{1,0:T(8,128)(2,1)S(1)} %get-tuple-element.61.v_ref, ...), custom_call_target="tpu_custom_call" | custom-call | tf_op jit(solution)/shard_map/pallas_call | solution.py:195
  114.5 2.0 %all_gather.13.both_ref = f32[512,128]{1,0:T(8,128)S(1)} all-gather(f32[256,128]{1,0:T(8,128)S(1)} %get-tuple-element.64), channel_id=1, replica_groups=mesh['y4'=2,'y2'=2,'y1'=2,'x2'=2,'x1'=2,'z3'=3,'z1'=2,'zh'=2,'core'=2] {..., dimensions={0}, use_global_device_ids=true | all-gather | bytes 393216 | tf_op jit(solution)/shard_map/all_gather | solution.py:265
  116.5 2.7 %shard_map.80 = (f32[256,128]{1,0:T(8,128)S(1)}, f32[256,128]{1,0:T(8,128)S(1)}, f32[256,128]{1,0:T(8,128)S(1)}, f32[256,128]{1,0:T(8,128)S(1)}) custom-call(s32[256]{0:T(256)S(1)} %get-tuple-element.58.refs_0_.lists_ref, f32[512,128]{1,0:T(8,128)S(1)} %all_gather.13.both_ref, bf16[256,128]{1,0:T(8,128)(2,1)S(1)} %constant_dynamic-slice_fusion.refs_1_.x_ref.sol_in, ...), custom_call_target="tpu_custom_call" | custom-call | tf_op jit(solution)/shard_map/pallas_call | solution.py:195
  119.2 2.0 %all_gather.14.both_ref = f32[512,128]{1,0:T(8,128)S(1)} all-gather(f32[256,128]{1,0:T(8,128)S(1)} %get-tuple-element.66), channel_id=1, replica_groups=mesh['y4'=2,'y2'=2,'y1'=2,'x2'=2,'x1'=2,'z3'=3,'z1'=2,'zh'=2,'core'=2] {..., dimensions={0}, use_global_device_ids=true | all-gather | bytes 393216 | tf_op jit(solution)/shard_map/all_gather | solution.py:265
  121.2 2.7 %shard_map.81 = (f32[256,128]{1,0:T(8,128)S(1)}, f32[256,128]{1,0:T(8,128)S(1)}, f32[256,128]{1,0:T(8,128)S(1)}, f32[256,128]{1,0:T(8,128)S(1)}) custom-call(s32[256]{0:T(256)S(1)} %get-tuple-element.58.refs_0_.lists_ref, f32[512,128]{1,0:T(8,128)S(1)} %all_gather.14.both_ref, f32[256,128]{1,0:T(8,128)S(1)} %get-tuple-element.67.sol_in, ...), custom_call_target="tpu_custom_call" | custom-call | tf_op jit(solution)/shard_map/pallas_call | solution.py:195
  124.0 2.0 %all_gather.15.both_ref = f32[512,128]{1,0:T(8,128)S(1)} all-gather(f32[256,128]{1,0:T(8,128)S(1)} %get-tuple-element.70), channel_id=1, replica_groups=mesh['y4'=2,'y2'=2,'y1'=2,'x2'=2,'x1'=2,'z3'=3,'z1'=2,'zh'=2,'core'=2] {..., dimensions={0}, use_global_device_ids=true | all-gather | bytes 393216 | tf_op jit(solution)/shard_map/all_gather | solution.py:265
  125.9 0.8 shard_map.82
  (6 shorter events, 0.0 us)
Async XLA Ops:
  0.6 33.4 %copy-start = (bf16[512,128]{1,0:T(8,128)(2,1)S(1)}, bf16[512,128]{1,0:T(8,128)(2,1)}, u32[]{:S(2)}) copy-start(bf16[512,128]{1,0:T(8,128)(2,1)} %param.8) | copy-start | bytes 393220
  3.5 26.2 %all-to-all-start.2 = ((bf16[12,48,128]{2,1,0:T(8,128)(2,1)}), bf16[12,48,128]{2,1,0:T(8,128)(2,1)S(1)}, u32[]{:S(2)}, u32[]{:S(2)}) async-start(bf16[12,48,128]{2,1,0:T(8,128)(2,1)} %broadcast_in_dim.40), calls=%async_computation.2 | async-start | bytes 294912 | tf_op jit(solution)/shard_map/all_to_all | solution.py:219
  29.7 78.1 %collective-permute-start = (bf16[32,128,128]{2,1,0:T(8,128)(2,1)S(1)}, bf16[32,128,128]{2,1,0:T(8,128)(2,1)S(1)}, u32[]{:S(2)}, u32[]{:S(2)}) collective-permute-start(bf16[32,128,128]{2,1,0:T(8,128)(2,1)S(1)} %select_convert_fusion.refs_3_.m0), channel_id=1, source_target_pairs={{0,2},{2,0},{1,3},{3,1},{4,6},{6,4},{5,7},{7,5},{8,10},{10,8},{9,1... | collective-permute-start | bytes 3145736 | tf_op jit(solution)/shard_map/ppermute | solution.py:223
  49.4 43.6 %all-to-all-start.1 = ((bf16[8,1536,128]{2,1,0:T(8,128)(2,1)}), bf16[8,1536,128]{2,1,0:T(8,128)(2,1)}, u32[]{:S(2)}, u32[]{:S(2)}) async-start(bf16[8,1536,128]{2,1,0:T(8,128)(2,1)} %broadcast_in_dim.7), calls=%async_computation.1 | async-start | bytes 6291456 | tf_op jit(solution)/shard_map/cond/branch_1_fun/all_to_all | solution.py:219

commit v4 on v3

--- a/solution.py
+++ b/solution.py
@@ -19,6 +19,7 @@
 K = 128
 NB = 32
 PIECE = 2 * BLK
+FIRST = 24
 STRIDE = NB
 TRIPS = 4 * STRIDE
 HALF = BLK // 2
@@ -34,14 +35,14 @@
         return carry
 
     lax.fori_loop(0, 4 * STRIDE, clear, 0, unroll=8)
-    longest = jnp.int32(0)
+    longest = sent = jnp.int32(0)
     for group, ids_ref in enumerate((own_ref, other_ref)):
         side = half if group == 0 else 1 - half
 
         def place(slot, ends, ids_ref=ids_ref, group=group, side=side):
             low, high = ends
             row = ids_ref[slot]
-            entry = slot
+            entry = low + high
             for k in range(2):
                 piece = 2 * ids_ref[NB + slot] + k
                 chip = lax.div(piece, 3)
@@ -59,9 +60,37 @@
             high = high + jnp.where(mine & upper, 1, 0)
             return low, high
 
-        low, high = lax.fori_loop(0, ids_ref[2 * NB], place, (jnp.int32(0), jnp.int32(0)))
+        count = ids_ref[2 * NB]
+        low, high = lax.fori_loop(0, count, place, (jnp.int32(0), jnp.int32(0)))
         longest = jnp.maximum(longest, jnp.maximum(low, high))
+        sent = jnp.maximum(sent, count - low - high if group == 0 else low + high)
     out_ref[TRIPS] = lax.div(longest + 1, 2)
+    out_ref[TRIPS + 1] = sent
+
+
+def sort_kernel(ids_ref, mask_ref, kept_ref, first_ref, rest_ref):
+    half = lax.axis_index("zh")
+
+    def place(slot, ends):
+        kept, sent = ends
+        mine = (ids_ref[slot] >> 1) == half
+        block = jnp.where(mask_ref[slot] > 0, CONFIDENCE, 0.0).astype(jnp.bfloat16)
+
+        @pl.when(mine)
+        def _():
+            kept_ref[kept] = block
+
+        @pl.when(jnp.logical_not(mine) & (sent < FIRST))
+        def _():
+            first_ref[sent] = block
+
+        @pl.when(jnp.logical_not(mine) & (sent >= FIRST))
+        def _():
+            rest_ref[sent - FIRST] = block
+
+        return kept + jnp.where(mine, 1, 0), sent + jnp.where(mine, 0, 1)
+
+    lax.fori_loop(0, ids_ref[2 * NB], place, (jnp.int32(0), jnp.int32(0)))
 
 
 def gram_of(v_ref):
@@ -127,15 +156,16 @@
     return jnp.dot(left, right, preferred_element_type=jnp.float32)
 
 
-def early_kernel(gravity, lists_ref, x_ref, v_in, m0, v_ref, gram_ref, part_ref):
-    v_ref[...] = v_in[...]
+def early_kernel(gravity, lists_ref, x_ref, v_in, m0, gram_ref, part_ref):
     gram = gravity * gram_of(v_in)
     gram_ref[...] = gram
     part_ref[...] = -exact_dot(x_ref[...].astype(jnp.float32), gram)
     add_sparse(lists_ref, x_ref, v_in, (m0, None), part_ref, True, (0,))
 
 
-def init_kernel(lists_ref, x_ref, v_ref, m1, part_in, part_ref):
+def init_kernel(lists_ref, x_ref, v_ref, first_ref, rest_ref, part_in, part_ref, m1):
+    m1[:FIRST] = first_ref[...]
+    m1[FIRST:] = rest_ref[...]
     part_ref[...] = part_in[...]
     add_sparse(lists_ref, x_ref, v_ref, (None, m1), part_ref, True, (1,))
 
@@ -228,43 +258,49 @@
     half = lax.axis_index("zh")
     gravity = K / (col_factors.shape[0] * 768)
 
-    live = (jnp.arange(NB) < block_counts[0, 0])[:, None, None]
-    own_masks = jnp.where(live & (block_masks[0, 0] > 0), CONFIDENCE, 0.0).astype(bf16)
     ids = jnp.concatenate(
         [block_rows[0, 0], block_cols[0, 0], jnp.broadcast_to(block_counts[0, 0], (2 * NB,))]
     )
     extra = jnp.broadcast_to(ids.astype(bf16)[None], (16, K))
     pieces = gather_stage(jnp.concatenate([col_factors, extra]), STAGES[0])
-    pieces, own_masks = lax.optimization_barrier((pieces, own_masks))
-    other_masks = swap(own_masks)
+    own_masks, sent_first, sent_rest = on_chip(
+        sort_kernel, (ids, block_masks[0, 0]), [((n, BLK, BLK), bf16) for n in (NB, FIRST, NB - FIRST)]
+    )
+    pieces, sent_first = lax.optimization_barrier((pieces, sent_first))
     pieces = pieces.reshape(12, 48, K)
     member = (1 - half) * 6 + lax.axis_index(("z3", "z1"))
     other_ids = lax.dynamic_index_in_dim(pieces[:, 32], member, 0, keepdims=False).astype(jnp.int32)
     pieces = pieces[:, :32].reshape(12 * 32, K)
 
-    def gathered(pieces, ids, other_ids):
-        lists = made_lists(ids, other_ids)
-        for axes in STAGES[1:]:
-            pieces = gather_stage(pieces, axes)
-        return pieces, lists
-
-    def nothing(pieces, ids, other_ids):
-        return jnp.zeros((32 * pieces.shape[0], K), bf16), jnp.zeros((2 * TRIPS,), jnp.int32)
-
-    rows_all, lists = lax.cond(block_counts[0, 0] > 0, gathered, nothing, pieces, ids, other_ids)
+    lists = made_lists(ids, other_ids)
+    got_first = swap(sent_first)
+    pieces, lists = lax.optimization_barrier((gather_stage(pieces, STAGES[1]), lists))
+
+    def gathered(pieces):
+        return gather_stage(pieces, STAGES[2])
+
+    def nothing(pieces):
+        return jnp.zeros((8 * pieces.shape[0], K), bf16)
+
+    rows_all = lax.cond(block_counts[0, 0] > 0, gathered, nothing, pieces)
+
     rows = lax.dynamic_slice_in_dim(start_rows, half * PIECE, PIECE, 0)
-    rows_all, gram, part = on_chip(
+    gram, part = on_chip(
         lambda *refs: early_kernel(gravity, *refs), (lists, rows, rows_all, own_masks),
-        [(rows_all.shape, bf16), ((K, K), f32), ((PIECE, K), f32)],
-    )
-    big = (rows_all, own_masks, other_masks, gram)
+        [((K, K), f32), ((PIECE, K), f32)],
+    )
     whole = ((PIECE, K), f32)
     low = (pltpu.VMEM((PIECE, K), bf16),)
 
     def both(part):
         return lax.all_gather(part, "core", axis=0, tiled=True)
 
-    (part,) = on_chip(init_kernel, (lists, rows, rows_all, other_masks, part), [whole])
+    got_first, sent_rest = lax.optimization_barrier((got_first, sent_rest))
+    got_rest = lax.cond(lists[TRIPS + 1] > FIRST, swap, jnp.zeros_like, sent_rest)
+    part, other_masks = on_chip(
+        init_kernel, (lists, rows, rows_all, got_first, got_rest, part), [whole, ((NB, BLK, BLK), bf16)]
+    )
+    big = (rows_all, own_masks, other_masks, gram)
     residual, part = on_chip(start_kernel, (lists, both(part), rows) + big, [whole] * 2, low)
     sol, direction = rows, residual
     for _ in range(ITERS - 1):

time: 127 us -> 127 us (level)
  the two profiles are of different devices: /device:TPU:61 before, /device:TPU:17 now
where the time goes in v4:
time: 127 us; the launch traced here: 126 us
  blocking collectives  57 us (45%)
  starting transfers between devices  26 us (20%)
  waiting for transfers between devices  18.8 us (15%)
  Pallas kernels  14.8 us (12%)
  local copies, waits for them, and re-layouts  5.52 us (4%)
  between operations  2.1 us (2%)
  other arithmetic  1.98 us (2%)
    all_to_all x1, blocking collectives, gather_stage(): lax.all_to_all(sent, axes, 0, 0, tiled=True).reshape(-1, block.shape[1])  40.3 us
    all_to_all x2, starting transfers between devices, gather_stage(): lax.all_to_all(sent, axes, 0, 0, tiled=True).reshape(-1, block.shape[1])  21.7 us
    all_to_all x2, waiting for transfers between devices, gather_stage(): lax.all_to_all(sent, axes, 0, 0, tiled=True).reshape(-1, block.shape[1])  18.8 us
    all_gather x4, blocking collectives, both(): return lax.all_gather(part, 'core', axis=0, tiled=True)  16.7 us
    pallas_call x7, Pallas kernels, on_chip(): pl.pallas_call(kernel, out_shape=[jax.ShapeDtypeStruct(shape, dtype) for...  13.1 us
    ppermute x1, starting transfers between devices, swap(): return lax.ppermute(value, 'zh', [(0, 1), (1, 0)])  4.31 us
  transfers between devices with their start and end apart: 3, of which 2 were waited for; matrix products, arithmetic and copies ran while one was open for 2% of the time, Pallas kernels for 6%

profile of v4, /device:TPU:17, one launch (start us, length us, event | category | flops | bytes accessed | tf_op | source)
XLA Modules:
  0.0 126.3 jit_solution(4204862240115797502)
XLA Ops:
  0.6 0.0 copy-start
  1.3 0.8 fusion
  2.1 0.7 pad_maximum_fusion
  2.8 0.7 broadcast_in_dim.14
  3.5 14.9 %all-to-all-start.1 = ((bf16[12,48,128]{2,1,0:T(8,128)(2,1)}), bf16[12,48,128]{2,1,0:T(8,128)(2,1)S(1)}, u32[]{:S(2)}, u32[]{:S(2)}) async-start(bf16[12,48,128]{2,1,0:T(8,128)(2,1)} %broadcast_in_dim.14), calls=%async_computation.1 | async-start | bytes 294912 | tf_op jit(solution)/shard_map/all_to_all | solution.py:249
  18.4 0.0 copy-start.1
  18.4 1.6 %copy-done.1 = s32[1,1,32,128,128]{4,3,2,1,0:T(8,128)S(1)} copy-done((s32[1,1,32,128,128]{4,3,2,1,0:T(8,128)S(1)}, s32[1,1,32,128,128]{4,3,2,1,0:T(8,128)}, u32[]{:S(2)}) %copy-start.1) | copy-done | bytes 2097176
  19.9 1.3 %shard_map.77 = (bf16[32,128,128]{2,1,0:T(8,128)(2,1)S(1)}, bf16[24,128,128]{2,1,0:T(8,128)(2,1)S(1)}, bf16[8,128,128]{2,1,0:T(8,128)(2,1)}) custom-call(s32[128]{0:T(128)S(1)} %get-tuple-element.57.ids_ref.own_ref, s32[32,128,128]{2,1,0:T(8,128)S(1)} %bitcast.15), custom_call_target="tpu_custom_call" | custom-call | tf_op jit(solution)/shard_map/pallas_call | solution.py:225
  21.3 8.4 %all-to-all-done.1 = bf16[12,48,128]{2,1,0:T(8,128)(2,1)S(1)} async-done(((bf16[12,48,128]{2,1,0:T(8,128)(2,1)}), bf16[12,48,128]{2,1,0:T(8,128)(2,1)S(1)}, u32[]{:S(2)}, u32[]{:S(2)}) %all-to-all-start.1) | async-done | bytes 147488 | tf_op jit(solution)/shard_map/all_to_all | solution.py:249
  29.7 4.3 %collective-permute-start.1 = (bf16[24,128,128]{2,1,0:T(8,128)(2,1)S(1)}, bf16[24,128,128]{2,1,0:T(8,128)(2,1)S(1)}, u32[]{:S(2)}, u32[]{:S(2)}) collective-permute-start(bf16[24,128,128]{2,1,0:T(8,128)(2,1)S(1)} %get-tuple-element.37), channel_id=1, source_target_pairs={{0,2},{2,0},{1,3},{3,1},{4,6},{6,4},{5,7},{7,5},{8,10},{10,8},{9,1... | collective-permute-start | bytes 2359304 | tf_op jit(solution)/shard_map/ppermute | solution.py:253
  34.0 0.8 broadcast_in_dim.32
  34.8 6.9 %all-to-all-start.2 = ((bf16[4,384,128]{2,1,0:T(8,128)(2,1)}), bf16[4,384,128]{2,1,0:T(8,128)(2,1)S(1)}, u32[]{:S(2)}, u32[]{:S(2)}) async-start(bf16[4,384,128]{2,1,0:T(8,128)(2,1)} %broadcast_in_dim.32), calls=%async_computation.2 | async-start | bytes 786432 | tf_op jit(solution)/shard_map/all_to_all | solution.py:249
  41.7 0.5 bitcast_convert_fusion.other_ref
  42.3 1.7 %shard_map.78.refs_0_.lists_ref = s32[256]{0:T(256)} custom-call(s32[128]{0:T(128)} %copy-done.3, s32[128]{0:T(128)} %bitcast_convert_fusion.other_ref), custom_call_target="tpu_custom_call" | custom-call | tf_op jit(solution)/shard_map/pallas_call | solution.py:236
  44.0 10.3 %all-to-all-done.2 = bf16[4,384,128]{2,1,0:T(8,128)(2,1)S(1)} async-done(((bf16[4,384,128]{2,1,0:T(8,128)(2,1)}), bf16[4,384,128]{2,1,0:T(8,128)(2,1)S(1)}, u32[]{:S(2)}, u32[]{:S(2)}) %all-to-all-start.2) | async-done | bytes 393248 | tf_op jit(solution)/shard_map/all_to_all | solution.py:249
  54.3 1.3 slice.11
  56.3 0.0 copy-start.2
  56.3 40.7 %conditional.2 = (bf16[12288,128]{1,0:T(8,128)(2,1)}) conditional(s32[]{:T(128)} %convert_element_type.24, () %tuple.24, bf16[1536,128]{1,0:T(8,128)(2,1)S(1)} %bitcast.17), branch_computations={%region_0.1_spmd, %region_1.2_spmd} | conditional | bytes 9830408 | solution.py:285
  56.3 0.4 broadcast_in_dim.0
  56.7 40.3 %all_to_all.14 = bf16[8,1536,128]{2,1,0:T(8,128)(2,1)} all-to-all(bf16[8,1536,128]{2,1,0:T(8,128)(2,1)S(1)} %broadcast_in_dim.0), channel_id=1, replica_groups=mesh['y4'=2,'y2'=2,'y1'=2,'x2'=2,'x1'=2,'z3'=3,'z1'=2,'zh'=2,'core'=2] {..., dimensions={0} | all-to-all | bytes 6291456 | tf_op jit(solution)/shard_map/cond/branch_1_fun/all_to_all | solution.py:249
  97.0 4.6 %shard_map.79 = (f32[128,128]{1,0:T(8,128)S(1)}, f32[256,128]{1,0:T(8,128)S(1)}) custom-call(s32[256]{0:T(256)S(1)} %copy-done.2, bf16[256,128]{1,0:T(8,128)(2,1)S(1)} %constant_dynamic-slice_fusion.refs_1_.x_ref.sol_in, bf16[12288,128]{1,0:T(8,128)(2,1)} %get-tuple-element.58.refs_2_.v_ref, bf16[32,128,128]{2,1,0:T(8,128)(2,1)S(1)} %get-tuple-element.41.refs_3_.m0), custom_call_target="tpu_custom_call" | custom-call | tf_op jit(solution)/shard_map/pallas_call | solution.py:225
  101.6 0.8 conditional.3
  101.6 0.7 broadcast.11
  102.3 2.5 %shard_map.80 = (f32[256,128]{1,0:T(8,128)S(1)}, bf16[32,128,128]{2,1,0:T(8,128)(2,1)S(1)}) custom-call(s32[256]{0:T(256)S(1)} %copy-done.2, bf16[256,128]{1,0:T(8,128)(2,1)S(1)} %constant_dynamic-slice_fusion.refs_1_.x_ref.sol_in, bf16[12288,128]{1,0:T(8,128)(2,1)} %get-tuple-element.58.refs_2_.v_ref, ...), custom_call_target="tpu_custom_call" | custom-call | tf_op jit(solution)/shard_map/pallas_call | solution.py:225
  104.8 6.6 %all_gather.12.both_ref = f32[512,128]{1,0:T(8,128)S(1)} all-gather(f32[256,128]{1,0:T(8,128)S(1)} %get-tuple-element.43), channel_id=1, replica_groups=mesh['y4'=2,'y2'=2,'y1'=2,'x2'=2,'x1'=2,'z3'=3,'z1'=2,'zh'=2,'core'=2] {..., dimensions={0}, use_global_device_ids=true | all-gather | bytes 393216 | tf_op jit(solution)/shard_map/all_gather | solution.py:296
  111.5 1.2 shard_map.81
  112.7 3.4 %all_gather.13.both_ref = f32[512,128]{1,0:T(8,128)S(1)} all-gather(f32[256,128]{1,0:T(8,128)S(1)} %get-tuple-element.46), channel_id=1, replica_groups=mesh['y4'=2,'y2'=2,'y1'=2,'x2'=2,'x1'=2,'z3'=3,'z1'=2,'zh'=2,'core'=2] {..., dimensions={0}, use_global_device_ids=true | all-gather | bytes 393216 | tf_op jit(solution)/shard_map/all_gather | solution.py:296
  116.0 1.4 %shard_map.82 = (f32[256,128]{1,0:T(8,128)S(1)}, f32[256,128]{1,0:T(8,128)S(1)}, f32[256,128]{1,0:T(8,128)S(1)}, f32[256,128]{1,0:T(8,128)S(1)}) custom-call(s32[256]{0:T(256)S(1)} %copy-done.2, f32[512,128]{1,0:T(8,128)S(1)} %all_gather.13.both_ref, bf16[256,128]{1,0:T(8,128)(2,1)S(1)} %constant_dynamic-slice_fusion.refs_1_.x_ref.sol_in, ...), custom_call_target="tpu_custom_call" | custom-call | tf_op jit(solution)/shard_map/pallas_call | solution.py:225
  117.4 3.4 %all_gather.14.both_ref = f32[512,128]{1,0:T(8,128)S(1)} all-gather(f32[256,128]{1,0:T(8,128)S(1)} %get-tuple-element.48), channel_id=1, replica_groups=mesh['y4'=2,'y2'=2,'y1'=2,'x2'=2,'x1'=2,'z3'=3,'z1'=2,'zh'=2,'core'=2] {..., dimensions={0}, use_global_device_ids=true | all-gather | bytes 393216 | tf_op jit(solution)/shard_map/all_gather | solution.py:296
  120.8 1.4 %shard_map.83 = (f32[256,128]{1,0:T(8,128)S(1)}, f32[256,128]{1,0:T(8,128)S(1)}, f32[256,128]{1,0:T(8,128)S(1)}, f32[256,128]{1,0:T(8,128)S(1)}) custom-call(s32[256]{0:T(256)S(1)} %copy-done.2, f32[512,128]{1,0:T(8,128)S(1)} %all_gather.14.both_ref, f32[256,128]{1,0:T(8,128)S(1)} %get-tuple-element.49.sol_in, f32[256,128]{1,0:T(8,128)S(1)} %get-tuple-element.50.res_in, ...), custom_call_target="tpu_custom_call" | custom-call | tf_op jit(solution)/shard_map/pallas_call | solution.py:225
  122.1 3.4 %all_gather.15.both_ref = f32[512,128]{1,0:T(8,128)S(1)} all-gather(f32[256,128]{1,0:T(8,128)S(1)} %get-tuple-element.52), channel_id=1, replica_groups=mesh['y4'=2,'y2'=2,'y1'=2,'x2'=2,'x1'=2,'z3'=3,'z1'=2,'zh'=2,'core'=2] {..., dimensions={0}, use_global_device_ids=true | all-gather | bytes 393216 | tf_op jit(solution)/shard_map/all_gather | solution.py:296
  125.5 0.8 shard_map.84
  (14 shorter events, 0.0 us)
Async XLA Ops:
  0.6 41.1 %copy-start = (bf16[512,128]{1,0:T(8,128)(2,1)S(1)}, bf16[512,128]{1,0:T(8,128)(2,1)}, u32[]{:S(2)}) copy-start(bf16[512,128]{1,0:T(8,128)(2,1)} %param.10) | copy-start | bytes 393220
  2.1 40.2 %copy-start.3 = (s32[128]{0:T(128)}, s32[128]{0:T(128)S(1)}, u32[]{:S(2)}) copy-start(s32[128]{0:T(128)S(1)} %get-tuple-element.57.ids_ref.own_ref) | copy-start | bytes 1540
  3.5 26.2 %all-to-all-start.1 = ((bf16[12,48,128]{2,1,0:T(8,128)(2,1)}), bf16[12,48,128]{2,1,0:T(8,128)(2,1)S(1)}, u32[]{:S(2)}, u32[]{:S(2)}) async-start(bf16[12,48,128]{2,1,0:T(8,128)(2,1)} %broadcast_in_dim.14), calls=%async_computation.1 | async-start | bytes 294912 | tf_op jit(solution)/shard_map/all_to_all | solution.py:249
  18.4 1.6 %copy-start.1 = (s32[1,1,32,128,128]{4,3,2,1,0:T(8,128)S(1)}, s32[1,1,32,128,128]{4,3,2,1,0:T(8,128)}, u32[]{:S(2)}) copy-start(s32[1,1,32,128,128]{4,3,2,1,0:T(8,128)} %param.14) | copy-start | bytes 6291460
  29.7 71.9 %collective-permute-start.1 = (bf16[24,128,128]{2,1,0:T(8,128)(2,1)S(1)}, bf16[24,128,128]{2,1,0:T(8,128)(2,1)S(1)}, u32[]{:S(2)}, u32[]{:S(2)}) collective-permute-start(bf16[24,128,128]{2,1,0:T(8,128)(2,1)S(1)} %get-tuple-element.37), channel_id=1, source_target_pairs={{0,2},{2,0},{1,3},{3,1},{4,6},{6,4},{5,7},{7,5},{8,10},{10,8},{9,1... | collective-permute-start | bytes 2359304 | tf_op jit(solution)/shard_map/ppermute | solution.py:253
  34.8 19.5 %all-to-all-start.2 = ((bf16[4,384,128]{2,1,0:T(8,128)(2,1)}), bf16[4,384,128]{2,1,0:T(8,128)(2,1)S(1)}, u32[]{:S(2)}, u32[]{:S(2)}) async-start(bf16[4,384,128]{2,1,0:T(8,128)(2,1)} %broadcast_in_dim.32), calls=%async_computation.2 | async-start | bytes 786432 | tf_op jit(solution)/shard_map/all_to_all | solution.py:249
  56.3 40.7 %copy-start.2 = (s32[256]{0:T(256)S(1)}, s32[256]{0:T(256)}, u32[]{:S(2)}) copy-start(s32[256]{0:T(256)} %shard_map.78.refs_0_.lists_ref) | copy-start | bytes 3076
  97.0 4.6 %copy-start.5 = (bf16[8,128,128]{2,1,0:T(8,128)(2,1)S(1)}, bf16[8,128,128]{2,1,0:T(8,128)(2,1)}, u32[]{:S(2)}) copy-start(bf16[8,128,128]{2,1,0:T(8,128)(2,1)} %get-tuple-element.40) | copy-start | bytes 786436
  102.3 9.1 %copy-start.4 = (bf16[12288,128]{1,0:T(8,128)(2,1)S(1)}, bf16[12288,128]{1,0:T(8,128)(2,1)}, u32[]{:S(2)}) copy-start(bf16[12288,128]{1,0:T(8,128)(2,1)} %get-tuple-element.58.refs_2_.v_ref) | copy-start | bytes 9437188

commit v5 on v4

--- a/solution.py
+++ b/solution.py
@@ -274,7 +274,8 @@
 
     lists = made_lists(ids, other_ids)
     got_first = swap(sent_first)
-    pieces, lists = lax.optimization_barrier((gather_stage(pieces, STAGES[1]), lists))
+    needs_rest = lists[TRIPS + 1] > FIRST
+    pieces, lists, needs_rest = lax.optimization_barrier((gather_stage(pieces, STAGES[1]), lists, needs_rest))
 
     def gathered(pieces):
         return gather_stage(pieces, STAGES[2])
@@ -296,7 +297,7 @@
         return lax.all_gather(part, "core", axis=0, tiled=True)
 
     got_first, sent_rest = lax.optimization_barrier((got_first, sent_rest))
-    got_rest = lax.cond(lists[TRIPS + 1] > FIRST, swap, jnp.zeros_like, sent_rest)
+    got_rest = lax.cond(needs_rest, swap, jnp.zeros_like, sent_rest)
     part, other_masks = on_chip(
         init_kernel, (lists, rows, rows_all, got_first, got_rest, part), [whole, ((NB, BLK, BLK), bf16)]
     )

time: 127 us -> 123 us (0.969)
  the two profiles are of different devices: /device:TPU:17 before, /device:TPU:1 now
where the time goes in v5:
time: 123 us; the launch traced here: 121 us
  blocking collectives  54.8 us (45%)
  starting transfers between devices  26.8 us (22%)
  Pallas kernels  15.5 us (13%)
  waiting for transfers between devices  14.5 us (12%)
  local copies, waits for them, and re-layouts  5.52 us (4%)
  between operations  2.09 us (2%)
  other arithmetic  1.98 us (2%)
    all_to_all x1, blocking collectives, gather_stage(): lax.all_to_all(sent, axes, 0, 0, tiled=True).reshape(-1, block.shape[1])  38.4 us
    all_to_all x2, starting transfers between devices, gather_stage(): lax.all_to_all(sent, axes, 0, 0, tiled=True).reshape(-1, block.shape[1])  22.5 us
    all_gather x4, blocking collectives, both(): return lax.all_gather(part, 'core', axis=0, tiled=True)  16.4 us
    all_to_all x2, waiting for transfers between devices, gather_stage(): lax.all_to_all(sent, axes, 0, 0, tiled=True).reshape(-1, block.shape[1])  14.5 us
    pallas_call x7, Pallas kernels, on_chip(): pl.pallas_call(kernel, out_shape=[jax.ShapeDtypeStruct(shape, dtype) for...  13.5 us
    ppermute x1, starting transfers between devices, swap(): return lax.ppermute(value, 'zh', [(0, 1), (1, 0)])  4.31 us
  transfers between devices with their start and end apart: 3, of which 2 were waited for; matrix products, arithmetic and copies ran while one was open for 2% of the time, Pallas kernels for 7%

profile of v5, /device:TPU:1, one launch (start us, length us, event | category | flops | bytes accessed | tf_op | source)
XLA Modules:
  0.0 121.3 jit_solution(4474408349760415157)
XLA Ops:
  0.6 0.0 copy-start
  1.3 0.8 fusion
  2.1 0.7 pad_maximum_fusion
  2.8 0.7 broadcast_in_dim.14
  3.5 15.7 %all-to-all-start.1 = ((bf16[12,48,128]{2,1,0:T(8,128)(2,1)}), bf16[12,48,128]{2,1,0:T(8,128)(2,1)S(1)}, u32[]{:S(2)}, u32[]{:S(2)}) async-start(bf16[12,48,128]{2,1,0:T(8,128)(2,1)} %broadcast_in_dim.14), calls=%async_computation.1 | async-start | bytes 294912 | tf_op jit(solution)/shard_map/all_to_all | solution.py:249
  19.2 0.0 copy-start.1
  19.2 1.6 %copy-done.1 = s32[1,1,32,128,128]{4,3,2,1,0:T(8,128)S(1)} copy-done((s32[1,1,32,128,128]{4,3,2,1,0:T(8,128)S(1)}, s32[1,1,32,128,128]{4,3,2,1,0:T(8,128)}, u32[]{:S(2)}) %copy-start.1) | copy-done | bytes 2097176
  20.8 1.7 %shard_map.77 = (bf16[32,128,128]{2,1,0:T(8,128)(2,1)S(1)}, bf16[24,128,128]{2,1,0:T(8,128)(2,1)S(1)}, bf16[8,128,128]{2,1,0:T(8,128)(2,1)}) custom-call(s32[128]{0:T(128)S(1)} %get-tuple-element.59.ids_ref.own_ref, s32[32,128,128]{2,1,0:T(8,128)S(1)} %bitcast.15), custom_call_target="tpu_custom_call" | custom-call | tf_op jit(solution)/shard_map/pallas_call | solution.py:225
  22.5 8.0 %all-to-all-done.1 = bf16[12,48,128]{2,1,0:T(8,128)(2,1)S(1)} async-done(((bf16[12,48,128]{2,1,0:T(8,128)(2,1)}), bf16[12,48,128]{2,1,0:T(8,128)(2,1)S(1)}, u32[]{:S(2)}, u32[]{:S(2)}) %all-to-all-start.1) | async-done | bytes 147488 | tf_op jit(solution)/shard_map/all_to_all | solution.py:249
  30.5 4.3 %collective-permute-start.1 = (bf16[24,128,128]{2,1,0:T(8,128)(2,1)S(1)}, bf16[24,128,128]{2,1,0:T(8,128)(2,1)S(1)}, u32[]{:S(2)}, u32[]{:S(2)}) collective-permute-start(bf16[24,128,128]{2,1,0:T(8,128)(2,1)S(1)} %get-tuple-element.38), channel_id=1, source_target_pairs={{0,2},{2,0},{1,3},{3,1},{4,6},{6,4},{5,7},{7,5},{8,10},{10,8},{9,1... | collective-permute-start | bytes 2359304 | tf_op jit(solution)/shard_map/ppermute | solution.py:253
  34.9 0.8 broadcast_in_dim.32
  35.7 6.8 %all-to-all-start.2 = ((bf16[4,384,128]{2,1,0:T(8,128)(2,1)}), bf16[4,384,128]{2,1,0:T(8,128)(2,1)S(1)}, u32[]{:S(2)}, u32[]{:S(2)}) async-start(bf16[4,384,128]{2,1,0:T(8,128)(2,1)} %broadcast_in_dim.32), calls=%async_computation.2 | async-start | bytes 786432 | tf_op jit(solution)/shard_map/all_to_all | solution.py:249
  42.5 0.5 bitcast_convert_fusion.other_ref
  43.0 2.1 %shard_map.78.refs_0_.lists_ref = s32[256]{0:T(256)} custom-call(s32[128]{0:T(128)} %copy-done.3, s32[128]{0:T(128)} %bitcast_convert_fusion.other_ref), custom_call_target="tpu_custom_call" | custom-call | tf_op jit(solution)/shard_map/pallas_call | solution.py:236
  45.1 1.3 %slice.11 = s32[1]{0:T(128)} slice(s32[256]{0:T(256)} %shard_map.78.refs_0_.lists_ref), slice={[129:130]} | slice | bytes 8 | tf_op jit(solution)/shard_map/slice | solution.py:277
  47.0 6.5 %all-to-all-done.2 = bf16[4,384,128]{2,1,0:T(8,128)(2,1)S(1)} async-done(((bf16[4,384,128]{2,1,0:T(8,128)(2,1)}), bf16[4,384,128]{2,1,0:T(8,128)(2,1)S(1)}, u32[]{:S(2)}, u32[]{:S(2)}) %all-to-all-start.2) | async-done | bytes 393248 | tf_op jit(solution)/shard_map/all_to_all | solution.py:249
  53.5 38.8 %conditional.2 = (bf16[12288,128]{1,0:T(8,128)(2,1)}) conditional(s32[]{:T(128)} %convert_element_type.21, () %tuple.24, bf16[1536,128]{1,0:T(8,128)(2,1)S(1)} %bitcast.17), branch_computations={%region_0.1_spmd, %region_1.2_spmd} | conditional | bytes 9830408 | solution.py:286
  53.5 0.4 broadcast_in_dim.0
  53.9 38.4 %all_to_all.14 = bf16[8,1536,128]{2,1,0:T(8,128)(2,1)} all-to-all(bf16[8,1536,128]{2,1,0:T(8,128)(2,1)S(1)} %broadcast_in_dim.0), channel_id=1, replica_groups=mesh['y4'=2,'y2'=2,'y1'=2,'x2'=2,'x1'=2,'z3'=3,'z1'=2,'zh'=2,'core'=2] {..., dimensions={0} | all-to-all | bytes 6291456 | tf_op jit(solution)/shard_map/cond/branch_1_fun/all_to_all | solution.py:249
  92.3 4.6 %shard_map.79 = (f32[128,128]{1,0:T(8,128)S(1)}, f32[256,128]{1,0:T(8,128)S(1)}) custom-call(s32[256]{0:T(256)S(1)} %copy-done.2, bf16[256,128]{1,0:T(8,128)(2,1)S(1)} %constant_dynamic-slice_fusion.refs_1_.x_ref.sol_in, bf16[12288,128]{1,0:T(8,128)(2,1)} %get-tuple-element.60.refs_2_.v_ref, bf16[32,128,128]{2,1,0:T(8,128)(2,1)S(1)} %get-tuple-element.43.refs_3_.m0), custom_call_target="tpu_custom_call" | custom-call | tf_op jit(solution)/shard_map/pallas_call | solution.py:225
  96.9 0.0 collective-permute-done.1.first_ref
  96.9 0.8 conditional.3
  96.9 0.7 broadcast.11
  97.7 2.5 %shard_map.80 = (f32[256,128]{1,0:T(8,128)S(1)}, bf16[32,128,128]{2,1,0:T(8,128)(2,1)S(1)}) custom-call(s32[256]{0:T(256)S(1)} %copy-done.2, bf16[256,128]{1,0:T(8,128)(2,1)S(1)} %constant_dynamic-slice_fusion.refs_1_.x_ref.sol_in, bf16[12288,128]{1,0:T(8,128)(2,1)} %get-tuple-element.60.refs_2_.v_ref, ...), custom_call_target="tpu_custom_call" | custom-call | tf_op jit(solution)/shard_map/pallas_call | solution.py:225
  100.2 7.7 %all_gather.12.both_ref = f32[512,128]{1,0:T(8,128)S(1)} all-gather(f32[256,128]{1,0:T(8,128)S(1)} %get-tuple-element.45), channel_id=1, replica_groups=mesh['y4'=2,'y2'=2,'y1'=2,'x2'=2,'x1'=2,'z3'=3,'z1'=2,'zh'=2,'core'=2] {..., dimensions={0}, use_global_device_ids=true | all-gather | bytes 393216 | tf_op jit(solution)/shard_map/all_gather | solution.py:297
  107.9 1.2 shard_map.81
  109.1 2.9 %all_gather.13.both_ref = f32[512,128]{1,0:T(8,128)S(1)} all-gather(f32[256,128]{1,0:T(8,128)S(1)} %get-tuple-element.48), channel_id=1, replica_groups=mesh['y4'=2,'y2'=2,'y1'=2,'x2'=2,'x1'=2,'z3'=3,'z1'=2,'zh'=2,'core'=2] {..., dimensions={0}, use_global_device_ids=true | all-gather | bytes 393216 | tf_op jit(solution)/shard_map/all_gather | solution.py:297
  112.0 1.4 %shard_map.82 = (f32[256,128]{1,0:T(8,128)S(1)}, f32[256,128]{1,0:T(8,128)S(1)}, f32[256,128]{1,0:T(8,128)S(1)}, f32[256,128]{1,0:T(8,128)S(1)}) custom-call(s32[256]{0:T(256)S(1)} %copy-done.2, f32[512,128]{1,0:T(8,128)S(1)} %all_gather.13.both_ref, bf16[256,128]{1,0:T(8,128)(2,1)S(1)} %constant_dynamic-slice_fusion.refs_1_.x_ref.sol_in, ...), custom_call_target="tpu_custom_call" | custom-call | tf_op jit(solution)/shard_map/pallas_call | solution.py:225
  113.4 2.9 %all_gather.14.both_ref = f32[512,128]{1,0:T(8,128)S(1)} all-gather(f32[256,128]{1,0:T(8,128)S(1)} %get-tuple-element.50), channel_id=1, replica_groups=mesh['y4'=2,'y2'=2,'y1'=2,'x2'=2,'x1'=2,'z3'=3,'z1'=2,'zh'=2,'core'=2] {..., dimensions={0}, use_global_device_ids=true | all-gather | bytes 393216 | tf_op jit(solution)/shard_map/all_gather | solution.py:297
  116.3 1.4 %shard_map.83 = (f32[256,128]{1,0:T(8,128)S(1)}, f32[256,128]{1,0:T(8,128)S(1)}, f32[256,128]{1,0:T(8,128)S(1)}, f32[256,128]{1,0:T(8,128)S(1)}) custom-call(s32[256]{0:T(256)S(1)} %copy-done.2, f32[512,128]{1,0:T(8,128)S(1)} %all_gather.14.both_ref, f32[256,128]{1,0:T(8,128)S(1)} %get-tuple-element.51.sol_in, f32[256,128]{1,0:T(8,128)S(1)} %get-tuple-element.52.res_in, ...), custom_call_target="tpu_custom_call" | custom-call | tf_op jit(solution)/shard_map/pallas_call | solution.py:225
  117.7 2.9 %all_gather.15.both_ref = f32[512,128]{1,0:T(8,128)S(1)} all-gather(f32[256,128]{1,0:T(8,128)S(1)} %get-tuple-element.54), channel_id=1, replica_groups=mesh['y4'=2,'y2'=2,'y1'=2,'x2'=2,'x1'=2,'z3'=3,'z1'=2,'zh'=2,'core'=2] {..., dimensions={0}, use_global_device_ids=true | all-gather | bytes 393216 | tf_op jit(solution)/shard_map/all_gather | solution.py:297
  120.6 0.8 shard_map.84
  (14 shorter events, 0.0 us)
Async XLA Ops:
  0.6 41.9 %copy-start = (bf16[512,128]{1,0:T(8,128)(2,1)S(1)}, bf16[512,128]{1,0:T(8,128)(2,1)}, u32[]{:S(2)}) copy-start(bf16[512,128]{1,0:T(8,128)(2,1)} %param.10) | copy-start | bytes 393220
  2.1 40.9 %copy-start.3 = (s32[128]{0:T(128)}, s32[128]{0:T(128)S(1)}, u32[]{:S(2)}) copy-start(s32[128]{0:T(128)S(1)} %get-tuple-element.59.ids_ref.own_ref) | copy-start | bytes 1540
  3.5 27.1 %all-to-all-start.1 = ((bf16[12,48,128]{2,1,0:T(8,128)(2,1)}), bf16[12,48,128]{2,1,0:T(8,128)(2,1)S(1)}, u32[]{:S(2)}, u32[]{:S(2)}) async-start(bf16[12,48,128]{2,1,0:T(8,128)(2,1)} %broadcast_in_dim.14), calls=%async_computation.1 | async-start | bytes 294912 | tf_op jit(solution)/shard_map/all_to_all | solution.py:249
  19.2 1.6 %copy-start.1 = (s32[1,1,32,128,128]{4,3,2,1,0:T(8,128)S(1)}, s32[1,1,32,128,128]{4,3,2,1,0:T(8,128)}, u32[]{:S(2)}) copy-start(s32[1,1,32,128,128]{4,3,2,1,0:T(8,128)} %param.14) | copy-start | bytes 6291460
  30.5 66.4 %collective-permute-start.1 = (bf16[24,128,128]{2,1,0:T(8,128)(2,1)S(1)}, bf16[24,128,128]{2,1,0:T(8,128)(2,1)S(1)}, u32[]{:S(2)}, u32[]{:S(2)}) collective-permute-start(bf16[24,128,128]{2,1,0:T(8,128)(2,1)S(1)} %get-tuple-element.38), channel_id=1, source_target_pairs={{0,2},{2,0},{1,3},{3,1},{4,6},{6,4},{5,7},{7,5},{8,10},{10,8},{9,1... | collective-permute-start | bytes 2359304 | tf_op jit(solution)/shard_map/ppermute | solution.py:253
  35.7 17.8 %all-to-all-start.2 = ((bf16[4,384,128]{2,1,0:T(8,128)(2,1)}), bf16[4,384,128]{2,1,0:T(8,128)(2,1)S(1)}, u32[]{:S(2)}, u32[]{:S(2)}) async-start(bf16[4,384,128]{2,1,0:T(8,128)(2,1)} %broadcast_in_dim.32), calls=%async_computation.2 | async-start | bytes 786432 | tf_op jit(solution)/shard_map/all_to_all | solution.py:249
  53.5 38.8 %copy-start.2 = (s32[256]{0:T(256)S(1)}, s32[256]{0:T(256)}, u32[]{:S(2)}) copy-start(s32[256]{0:T(256)} %shard_map.78.refs_0_.lists_ref) | copy-start | bytes 3076
  92.3 4.6 %copy-start.5 = (bf16[8,128,128]{2,1,0:T(8,128)(2,1)S(1)}, bf16[8,128,128]{2,1,0:T(8,128)(2,1)}, u32[]{:S(2)}) copy-start(bf16[8,128,128]{2,1,0:T(8,128)(2,1)} %get-tuple-element.42) | copy-start | bytes 786436
  97.7 10.3 %copy-start.4 = (bf16[12288,128]{1,0:T(8,128)(2,1)S(1)}, bf16[12288,128]{1,0:T(8,128)(2,1)}, u32[]{:S(2)}) copy-start(bf16[12288,128]{1,0:T(8,128)(2,1)} %get-tuple-element.60.refs_2_.v_ref) | copy-start | bytes 9437188

commit v6 on v5

--- a/solution.py
+++ b/solution.py
@@ -297,7 +297,7 @@
         return lax.all_gather(part, "core", axis=0, tiled=True)
 
     got_first, sent_rest = lax.optimization_barrier((got_first, sent_rest))
-    got_rest = lax.cond(needs_rest, swap, jnp.zeros_like, sent_rest)
+    got_rest = lax.cond(needs_rest, swap, lambda unused: unused, sent_rest)
     part, other_masks = on_chip(
         init_kernel, (lists, rows, rows_all, got_first, got_rest, part), [whole, ((NB, BLK, BLK), bf16)]
     )

time: 123 us -> 121 us (0.984)
  blocking collectives: 54.8 us -> 50.6 us
  Pallas kernels: 15.5 us -> 17.7 us
    all_gather x4, blocking collectives: 16.4 us -> 12.2 us  [both(): return lax.all_gather(part, 'core', axis=0, tiled=True)]
    pallas_call x7, Pallas kernels: 13.5 us -> 15.5 us  [on_chip(): pl.pallas_call(kernel, out_shape=[jax.ShapeDtypeStruct(shape, dtype) for...]
  transfers between devices with their start and end apart: 3 -> 3, of which waited for: 2 -> 2; matrix products, arithmetic and copies ran while one was open for 2% -> 3% of each run, Pallas kernels for 7% -> 7%
where the time goes in v6:
time: 121 us; the launch traced here: 118 us
  blocking collectives  50.6 us (42%)
  starting transfers between devices  26.8 us (22%)
  Pallas kernels  17.7 us (15%)
  waiting for transfers between devices  14.5 us (12%)
  local copies, waits for them, and re-layouts  4.78 us (4%)
  between operations  2.11 us (2%)
  other arithmetic  1.98 us (2%)
    all_to_all x1, blocking collectives, gather_stage(): lax.all_to_all(sent, axes, 0, 0, tiled=True).reshape(-1, block.shape[1])  38.4 us
    all_to_all x2, starting transfers between devices, gather_stage(): lax.all_to_all(sent, axes, 0, 0, tiled=True).reshape(-1, block.shape[1])  22.5 us
    pallas_call x7, Pallas kernels, on_chip(): pl.pallas_call(kernel, out_shape=[jax.ShapeDtypeStruct(shape, dtype) for...  15.5 us
    all_to_all x2, waiting for transfers between devices, gather_stage(): lax.all_to_all(sent, axes, 0, 0, tiled=True).reshape(-1, block.shape[1])  14.5 us
    all_gather x4, blocking collectives, both(): return lax.all_gather(part, 'core', axis=0, tiled=True)  12.2 us
    ppermute x1, starting transfers between devices, swap(): return lax.ppermute(value, 'zh', [(0, 1), (1, 0)])  4.31 us
  transfers between devices with their start and end apart: 3, of which 2 were waited for; matrix products, arithmetic and copies ran while one was open for 3% of the time, Pallas kernels for 7%

profile of v6, /device:TPU:1, one launch (start us, length us, event | category | flops | bytes accessed | tf_op | source)
XLA Modules:
  0.0 118.5 jit_solution(5768243566096708407)
XLA Ops:
  0.6 0.0 copy-start
  1.3 0.8 fusion
  2.1 0.7 pad_maximum_fusion
  2.8 0.7 broadcast_in_dim.14
  3.5 15.7 %all-to-all-start.1 = ((bf16[12,48,128]{2,1,0:T(8,128)(2,1)}), bf16[12,48,128]{2,1,0:T(8,128)(2,1)S(1)}, u32[]{:S(2)}, u32[]{:S(2)}) async-start(bf16[12,48,128]{2,1,0:T(8,128)(2,1)} %broadcast_in_dim.14), calls=%async_computation.1 | async-start | bytes 294912 | tf_op jit(solution)/shard_map/all_to_all | solution.py:249
  19.2 0.0 copy-start.1
  19.2 1.6 %copy-done.1 = s32[1,1,32,128,128]{4,3,2,1,0:T(8,128)S(1)} copy-done((s32[1,1,32,128,128]{4,3,2,1,0:T(8,128)S(1)}, s32[1,1,32,128,128]{4,3,2,1,0:T(8,128)}, u32[]{:S(2)}) %copy-start.1) | copy-done | bytes 2097176
  20.8 1.6 %shard_map.77 = (bf16[32,128,128]{2,1,0:T(8,128)(2,1)S(1)}, bf16[24,128,128]{2,1,0:T(8,128)(2,1)S(1)}, bf16[8,128,128]{2,1,0:T(8,128)(2,1)}) custom-call(s32[128]{0:T(128)S(1)} %get-tuple-element.60.ids_ref.own_ref, s32[32,128,128]{2,1,0:T(8,128)S(1)} %bitcast.15), custom_call_target="tpu_custom_call" | custom-call | tf_op jit(solution)/shard_map/pallas_call | solution.py:225
  22.4 8.1 %all-to-all-done.1 = bf16[12,48,128]{2,1,0:T(8,128)(2,1)S(1)} async-done(((bf16[12,48,128]{2,1,0:T(8,128)(2,1)}), bf16[12,48,128]{2,1,0:T(8,128)(2,1)S(1)}, u32[]{:S(2)}, u32[]{:S(2)}) %all-to-all-start.1) | async-done | bytes 147488 | tf_op jit(solution)/shard_map/all_to_all | solution.py:249
  30.5 4.3 %collective-permute-start.1 = (bf16[24,128,128]{2,1,0:T(8,128)(2,1)S(1)}, bf16[24,128,128]{2,1,0:T(8,128)(2,1)S(1)}, u32[]{:S(2)}, u32[]{:S(2)}) collective-permute-start(bf16[24,128,128]{2,1,0:T(8,128)(2,1)S(1)} %get-tuple-element.39), channel_id=1, source_target_pairs={{0,2},{2,0},{1,3},{3,1},{4,6},{6,4},{5,7},{7,5},{8,10},{10,8},{9,1... | collective-permute-start | bytes 2359304 | tf_op jit(solution)/shard_map/ppermute | solution.py:253
  34.9 0.8 broadcast_in_dim.32
  35.7 6.8 %all-to-all-start.2 = ((bf16[4,384,128]{2,1,0:T(8,128)(2,1)}), bf16[4,384,128]{2,1,0:T(8,128)(2,1)S(1)}, u32[]{:S(2)}, u32[]{:S(2)}) async-start(bf16[4,384,128]{2,1,0:T(8,128)(2,1)} %broadcast_in_dim.32), calls=%async_computation.2 | async-start | bytes 786432 | tf_op jit(solution)/shard_map/all_to_all | solution.py:249
  42.5 0.0 copy-done
  42.5 0.5 bitcast_convert_fusion.other_ref
  43.0 2.2 %shard_map.78.refs_0_.lists_ref = s32[256]{0:T(256)} custom-call(s32[128]{0:T(128)} %copy-done.3, s32[128]{0:T(128)} %bitcast_convert_fusion.other_ref), custom_call_target="tpu_custom_call" | custom-call | tf_op jit(solution)/shard_map/pallas_call | solution.py:236
  45.2 1.3 %slice.11 = s32[1]{0:T(128)} slice(s32[256]{0:T(256)} %shard_map.78.refs_0_.lists_ref), slice={[129:130]} | slice | bytes 8 | tf_op jit(solution)/shard_map/slice | solution.py:277
  47.2 6.3 %all-to-all-done.2 = bf16[4,384,128]{2,1,0:T(8,128)(2,1)S(1)} async-done(((bf16[4,384,128]{2,1,0:T(8,128)(2,1)}), bf16[4,384,128]{2,1,0:T(8,128)(2,1)S(1)}, u32[]{:S(2)}, u32[]{:S(2)}) %all-to-all-start.2) | async-done | bytes 393248 | tf_op jit(solution)/shard_map/all_to_all | solution.py:249
  53.5 38.8 %conditional.2 = (bf16[12288,128]{1,0:T(8,128)(2,1)}) conditional(s32[]{:T(128)} %convert_element_type.21, () %tuple.24, bf16[1536,128]{1,0:T(8,128)(2,1)S(1)} %bitcast.17), branch_computations={%region_0.1_spmd, %region_1.2_spmd} | conditional | bytes 9830408 | solution.py:286
  53.5 0.4 broadcast_in_dim.0
  53.9 38.4 %all_to_all.14 = bf16[8,1536,128]{2,1,0:T(8,128)(2,1)} all-to-all(bf16[8,1536,128]{2,1,0:T(8,128)(2,1)S(1)} %broadcast_in_dim.0), channel_id=1, replica_groups=mesh['y4'=2,'y2'=2,'y1'=2,'x2'=2,'x1'=2,'z3'=3,'z1'=2,'zh'=2,'core'=2] {..., dimensions={0} | all-to-all | bytes 6291456 | tf_op jit(solution)/shard_map/cond/branch_1_fun/all_to_all | solution.py:249
  92.3 5.0 %shard_map.79 = (f32[128,128]{1,0:T(8,128)S(1)}, f32[256,128]{1,0:T(8,128)S(1)}) custom-call(s32[256]{0:T(256)S(1)} %copy-done.2, bf16[256,128]{1,0:T(8,128)(2,1)S(1)} %constant_dynamic-slice_fusion.refs_1_.x_ref.sol_in, bf16[12288,128]{1,0:T(8,128)(2,1)} %get-tuple-element.61.refs_2_.v_ref, bf16[32,128,128]{2,1,0:T(8,128)(2,1)S(1)} %get-tuple-element.44.refs_3_.m0), custom_call_target="tpu_custom_call" | custom-call | tf_op jit(solution)/shard_map/pallas_call | solution.py:225
  97.3 0.0 collective-permute-done.1.first_ref
  97.3 0.0 copy-start.4
  97.3 2.9 %shard_map.80 = (f32[256,128]{1,0:T(8,128)S(1)}, bf16[32,128,128]{2,1,0:T(8,128)(2,1)S(1)}) custom-call(s32[256]{0:T(256)S(1)} %copy-done.2, bf16[256,128]{1,0:T(8,128)(2,1)S(1)} %constant_dynamic-slice_fusion.refs_1_.x_ref.sol_in, bf16[12288,128]{1,0:T(8,128)(2,1)} %get-tuple-element.61.refs_2_.v_ref, ...), custom_call_target="tpu_custom_call" | custom-call | tf_op jit(solution)/shard_map/pallas_call | solution.py:225
  100.2 6.2 %all_gather.12.both_ref = f32[512,128]{1,0:T(8,128)S(1)} all-gather(f32[256,128]{1,0:T(8,128)S(1)} %get-tuple-element.46), channel_id=1, replica_groups=mesh['y4'=2,'y2'=2,'y1'=2,'x2'=2,'x1'=2,'z3'=3,'z1'=2,'zh'=2,'core'=2] {..., dimensions={0}, use_global_device_ids=true | all-gather | bytes 393216 | tf_op jit(solution)/shard_map/all_gather | solution.py:297
  106.4 1.7 %shard_map.81 = (f32[256,128]{1,0:T(8,128)S(1)}, f32[256,128]{1,0:T(8,128)S(1)}) custom-call(s32[256]{0:T(256)S(1)} %copy-done.2, f32[512,128]{1,0:T(8,128)S(1)} %all_gather.12.both_ref, bf16[256,128]{1,0:T(8,128)(2,1)S(1)} %constant_dynamic-slice_fusion.refs_1_.x_ref.sol_in, bf16[12288,128]{1,0:T(8,128)(2,1)S(1)} %copy-done.4, ...), custom_call_target="tpu_custom_call" | custom-call | tf_op jit(solution)/shard_map/pallas_call | solution.py:225
  108.1 2.0 %all_gather.13.both_ref = f32[512,128]{1,0:T(8,128)S(1)} all-gather(f32[256,128]{1,0:T(8,128)S(1)} %get-tuple-element.49), channel_id=1, replica_groups=mesh['y4'=2,'y2'=2,'y1'=2,'x2'=2,'x1'=2,'z3'=3,'z1'=2,'zh'=2,'core'=2] {..., dimensions={0}, use_global_device_ids=true | all-gather | bytes 393216 | tf_op jit(solution)/shard_map/all_gather | solution.py:297
  110.1 1.8 %shard_map.82 = (f32[256,128]{1,0:T(8,128)S(1)}, f32[256,128]{1,0:T(8,128)S(1)}, f32[256,128]{1,0:T(8,128)S(1)}, f32[256,128]{1,0:T(8,128)S(1)}) custom-call(s32[256]{0:T(256)S(1)} %copy-done.2, f32[512,128]{1,0:T(8,128)S(1)} %all_gather.13.both_ref, bf16[256,128]{1,0:T(8,128)(2,1)S(1)} %constant_dynamic-slice_fusion.refs_1_.x_ref.sol_in, ...), custom_call_target="tpu_custom_call" | custom-call | tf_op jit(solution)/shard_map/pallas_call | solution.py:225
  111.9 2.0 %all_gather.14.both_ref = f32[512,128]{1,0:T(8,128)S(1)} all-gather(f32[256,128]{1,0:T(8,128)S(1)} %get-tuple-element.51), channel_id=1, replica_groups=mesh['y4'=2,'y2'=2,'y1'=2,'x2'=2,'x1'=2,'z3'=3,'z1'=2,'zh'=2,'core'=2] {..., dimensions={0}, use_global_device_ids=true | all-gather | bytes 393216 | tf_op jit(solution)/shard_map/all_gather | solution.py:297
  113.9 1.8 %shard_map.83 = (f32[256,128]{1,0:T(8,128)S(1)}, f32[256,128]{1,0:T(8,128)S(1)}, f32[256,128]{1,0:T(8,128)S(1)}, f32[256,128]{1,0:T(8,128)S(1)}) custom-call(s32[256]{0:T(256)S(1)} %copy-done.2, f32[512,128]{1,0:T(8,128)S(1)} %all_gather.14.both_ref, f32[256,128]{1,0:T(8,128)S(1)} %get-tuple-element.52.sol_in, f32[256,128]{1,0:T(8,128)S(1)} %get-tuple-element.53.res_in, ...), custom_call_target="tpu_custom_call" | custom-call | tf_op jit(solution)/shard_map/pallas_call | solution.py:225
  115.7 2.0 %all_gather.15.both_ref = f32[512,128]{1,0:T(8,128)S(1)} all-gather(f32[256,128]{1,0:T(8,128)S(1)} %get-tuple-element.55), channel_id=1, replica_groups=mesh['y4'=2,'y2'=2,'y1'=2,'x2'=2,'x1'=2,'z3'=3,'z1'=2,'zh'=2,'core'=2] {..., dimensions={0}, use_global_device_ids=true | all-gather | bytes 393216 | tf_op jit(solution)/shard_map/all_gather | solution.py:297
  117.7 0.8 shard_map.84
  (13 shorter events, 0.1 us)
Async XLA Ops:
  0.6 41.9 %copy-start = (bf16[512,128]{1,0:T(8,128)(2,1)S(1)}, bf16[512,128]{1,0:T(8,128)(2,1)}, u32[]{:S(2)}) copy-start(bf16[512,128]{1,0:T(8,128)(2,1)} %param.10) | copy-start | bytes 393220
  2.1 40.9 %copy-start.3 = (s32[128]{0:T(128)}, s32[128]{0:T(128)S(1)}, u32[]{:S(2)}) copy-start(s32[128]{0:T(128)S(1)} %get-tuple-element.60.ids_ref.own_ref) | copy-start | bytes 1540
  3.5 27.1 %all-to-all-start.1 = ((bf16[12,48,128]{2,1,0:T(8,128)(2,1)}), bf16[12,48,128]{2,1,0:T(8,128)(2,1)S(1)}, u32[]{:S(2)}, u32[]{:S(2)}) async-start(bf16[12,48,128]{2,1,0:T(8,128)(2,1)} %broadcast_in_dim.14), calls=%async_computation.1 | async-start | bytes 294912 | tf_op jit(solution)/shard_map/all_to_all | solution.py:249
  19.2 1.6 %copy-start.1 = (s32[1,1,32,128,128]{4,3,2,1,0:T(8,128)S(1)}, s32[1,1,32,128,128]{4,3,2,1,0:T(8,128)}, u32[]{:S(2)}) copy-start(s32[1,1,32,128,128]{4,3,2,1,0:T(8,128)} %param.14) | copy-start | bytes 6291460
  30.5 66.7 %collective-permute-start.1 = (bf16[24,128,128]{2,1,0:T(8,128)(2,1)S(1)}, bf16[24,128,128]{2,1,0:T(8,128)(2,1)S(1)}, u32[]{:S(2)}, u32[]{:S(2)}) collective-permute-start(bf16[24,128,128]{2,1,0:T(8,128)(2,1)S(1)} %get-tuple-element.39), channel_id=1, source_target_pairs={{0,2},{2,0},{1,3},{3,1},{4,6},{6,4},{5,7},{7,5},{8,10},{10,8},{9,1... | collective-permute-start | bytes 2359304 | tf_op jit(solution)/shard_map/ppermute | solution.py:253
  35.7 17.8 %all-to-all-start.2 = ((bf16[4,384,128]{2,1,0:T(8,128)(2,1)}), bf16[4,384,128]{2,1,0:T(8,128)(2,1)S(1)}, u32[]{:S(2)}, u32[]{:S(2)}) async-start(bf16[4,384,128]{2,1,0:T(8,128)(2,1)} %broadcast_in_dim.32), calls=%async_computation.2 | async-start | bytes 786432 | tf_op jit(solution)/shard_map/all_to_all | solution.py:249
  53.5 38.8 %copy-start.2 = (s32[256]{0:T(256)S(1)}, s32[256]{0:T(256)}, u32[]{:S(2)}) copy-start(s32[256]{0:T(256)} %shard_map.78.refs_0_.lists_ref) | copy-start | bytes 3076
  92.3 5.0 %copy-start.5 = (bf16[8,128,128]{2,1,0:T(8,128)(2,1)S(1)}, bf16[8,128,128]{2,1,0:T(8,128)(2,1)}, u32[]{:S(2)}) copy-start(bf16[8,128,128]{2,1,0:T(8,128)(2,1)} %get-tuple-element.43) | copy-start | bytes 786436
  97.3 9.1 %copy-start.4 = (bf16[12288,128]{1,0:T(8,128)(2,1)S(1)}, bf16[12288,128]{1,0:T(8,128)(2,1)}, u32[]{:S(2)}) copy-start(bf16[12288,128]{1,0:T(8,128)(2,1)} %get-tuple-element.61.refs_2_.v_ref) | copy-start | bytes 9437188
